TPU v7x, 32 devices: a whole 2x2x4 slice. The times are simulated.
32 devices in a mesh: views: 4 (over y, x), tiles: 8 (over z, core).
Axes of the slice: x: 2, y: 2, z: 4, core: 2. Of those that a mesh axis runs over, the one named last changes fastest.
Arguments:
- params: float32 [59, 4096], P(None, ('views', 'tiles')), as said below
- first_moment: float32 [59, 4096], P(None, ('views', 'tiles')), may hold values from -6 to 6
- second_moment: float32 [59, 4096], P(None, ('views', 'tiles')), may hold values from 0.5 to 20
- cameras: float32 [4, 6], replicated, may hold values from -0.02 to 0.02
- target: float32 [4, 128, 3, 256], P('views', 'tiles'), may hold values from 0 to 1
- lists: int32 [4, 128, 256], P('views', 'tiles'), may hold values from 0 to 4095, as said below
- lengths: int32 [4, 128], P('views', 'tiles'), may hold values from 32 to 256
Outputs:
- new_params: float32 [59, 4096], P(None, ('views', 'tiles'))
- new_first: float32 [59, 4096], P(None, ('views', 'tiles'))
- new_second: float32 [59, 4096], P(None, ('views', 'tiles'))
Inputs may be any that keep to these rules, and one draw needn't show every extreme that they name: Each entry names a Gaussian by its column in params. The lists of the 16 tiles that one device holds (live entries or not) have exactly 128 entries in the columns of each device's shard of params. `params`: the quaternion's first entry is at least 0.6, the means lie in front of every camera, and the opacity logits are at most -2.
All inputs are finite; a program needn't handle non-finite values.
Results may differ from a plain program's by a relative error of at most 0.0003.
Values sent between devices are 32-bit elements; how exact they have to be, the bound alone decides.
A program may use at most 128 MiB of HBM per device.

v0:
```python
import jax
import jax.numpy as jnp
import numpy as np
from jax import lax
from jax.sharding import PartitionSpec as P

TILE_SIDE = 16
TILE_COLS = 32
ADAM_STEP = 1000


sh_zero = 0.28209479177387814
sh_first = 0.4886025119029199
sh_second = (
    1.0925484305920792,
    -1.0925484305920792,
    0.31539156525252005,
    -1.0925484305920792,
    0.5462742152960396,
)
sh_third = (
    -0.5900435899266435,
    2.890611442640554,
    -0.4570457994644658,
    0.3731763325901154,
    -0.4570457994644658,
    1.445305721320277,
    -0.5900435899266435,
)
beta_one = 0.9
beta_two = 0.999
adam_eps = 1e-15
learning = np.concatenate(
    [
        np.full(3, 0.00016),
        np.full(3, 0.005),
        np.full(4, 0.001),
        np.full(1, 0.05),
        np.full(3, 0.0025),
        np.full(45, 0.000125),
    ]
).astype(np.float32)[:, None]


def matmul_three(left, right):
    return [
        [
            left[row_at][0] * right[0][col_at]
            + left[row_at][1] * right[1][col_at]
            + left[row_at][2] * right[2][col_at]
            for col_at in range(3)
        ]
        for row_at in range(3)
    ]


def camera_rotation(camera):
    cos_a, sin_a = (jnp.cos(camera[0]), jnp.sin(camera[0]))
    cos_b, sin_b = (jnp.cos(camera[1]), jnp.sin(camera[1]))
    cos_c, sin_c = (jnp.cos(camera[2]), jnp.sin(camera[2]))
    around_x = [[1.0, 0.0, 0.0], [0.0, cos_a, -sin_a], [0.0, sin_a, cos_a]]
    around_y = [[cos_b, 0.0, sin_b], [0.0, 1.0, 0.0], [-sin_b, 0.0, cos_b]]
    around_z = [[cos_c, -sin_c, 0.0], [sin_c, cos_c, 0.0], [0.0, 0.0, 1.0]]
    return matmul_three(around_z, matmul_three(around_y, around_x))


def sh_basis(along_x, along_y, along_z):
    square_x, square_y, square_z = (along_x * along_x, along_y * along_y, along_z * along_z)
    both_xy, both_yz, both_xz = (along_x * along_y, along_y * along_z, along_x * along_z)
    return [
        sh_zero + 0.0 * along_x,
        -sh_first * along_y,
        sh_first * along_z,
        -sh_first * along_x,
        sh_second[0] * both_xy,
        sh_second[1] * both_yz,
        sh_second[2] * (2.0 * square_z - square_x - square_y),
        sh_second[3] * both_xz,
        sh_second[4] * (square_x - square_y),
        sh_third[0] * along_y * (3.0 * square_x - square_y),
        sh_third[1] * both_xy * along_z,
        sh_third[2] * along_y * (4.0 * square_z - square_x - square_y),
        sh_third[3] * along_z * (2.0 * square_z - 3.0 * square_x - 3.0 * square_y),
        sh_third[4] * along_x * (4.0 * square_z - square_x - square_y),
        sh_third[5] * along_z * (square_x - square_y),
        sh_third[6] * along_x * (square_x - 3.0 * square_y),
    ]


def project(params, camera, focal_len, center_x, center_y):
    rotation = camera_rotation(camera)
    means = [params[0], params[1], params[2]]
    point = [
        rotation[axis_at][0] * means[0]
        + rotation[axis_at][1] * means[1]
        + rotation[axis_at][2] * means[2]
        + camera[3 + axis_at]
        for axis_at in range(3)
    ]
    inverse_z = 1.0 / point[2]
    screen_u = focal_len * point[0] * inverse_z + center_x
    screen_v = focal_len * point[1] * inverse_z + center_y
    scales = jnp.exp(params[3:6])
    unit_quat = params[6:10] * lax.rsqrt(jnp.sum(params[6:10] * params[6:10], axis=0))
    real_part, imag_x, imag_y, imag_z = (unit_quat[0], unit_quat[1], unit_quat[2], unit_quat[3])
    spin = [
        [
            1.0 - 2.0 * (imag_y * imag_y + imag_z * imag_z),
            2.0 * (imag_x * imag_y - real_part * imag_z),
            2.0 * (imag_x * imag_z + real_part * imag_y),
        ],
        [
            2.0 * (imag_x * imag_y + real_part * imag_z),
            1.0 - 2.0 * (imag_x * imag_x + imag_z * imag_z),
            2.0 * (imag_y * imag_z - real_part * imag_x),
        ],
        [
            2.0 * (imag_x * imag_z - real_part * imag_y),
            2.0 * (imag_y * imag_z + real_part * imag_x),
            1.0 - 2.0 * (imag_x * imag_x + imag_y * imag_y),
        ],
    ]
    turned = matmul_three(rotation, spin)
    shaped = [
        [turned[row_at][col_at] * scales[col_at] for col_at in range(3)] for row_at in range(3)
    ]
    near_x = [
        focal_len * inverse_z * shaped[0][col_at]
        - focal_len * point[0] * inverse_z * inverse_z * shaped[2][col_at]
        for col_at in range(3)
    ]
    near_y = [
        focal_len * inverse_z * shaped[1][col_at]
        - focal_len * point[1] * inverse_z * inverse_z * shaped[2][col_at]
        for col_at in range(3)
    ]
    cov_a = near_x[0] * near_x[0] + near_x[1] * near_x[1] + near_x[2] * near_x[2] + 0.3
    cov_b = near_x[0] * near_y[0] + near_x[1] * near_y[1] + near_x[2] * near_y[2]
    cov_c = near_y[0] * near_y[0] + near_y[1] * near_y[1] + near_y[2] * near_y[2] + 0.3
    determinant = cov_a * cov_c - cov_b * cov_b
    offset = [
        means[axis_at]
        + rotation[0][axis_at] * camera[3]
        + rotation[1][axis_at] * camera[4]
        + rotation[2][axis_at] * camera[5]
        for axis_at in range(3)
    ]
    inverse_len = lax.rsqrt(offset[0] * offset[0] + offset[1] * offset[1] + offset[2] * offset[2])
    basis = sh_basis(offset[0] * inverse_len, offset[1] * inverse_len, offset[2] * inverse_len)
    colors = [
        0.5 + sum((basis[coef_at] * params[11 + 3 * coef_at + channel] for coef_at in range(16)))
        for channel in range(3)
    ]
    opacity = jax.nn.sigmoid(params[10])
    return jnp.stack(
        [
            screen_u,
            screen_v,
            cov_c / determinant,
            -cov_b / determinant,
            cov_a / determinant,
            opacity,
            colors[0],
            colors[1],
            colors[2],
        ]
    )


def composite(picked, lengths, target, first_tile):
    tile_count = picked.shape[1]
    list_size = picked.shape[2]
    tile_ids = first_tile + jnp.arange(tile_count, dtype=jnp.int32)
    pixel_ids = jnp.arange(TILE_SIDE * TILE_SIDE, dtype=jnp.int32)
    pixel_x = (tile_ids % TILE_COLS * TILE_SIDE)[:, None] + (pixel_ids % TILE_SIDE)[None, :]
    pixel_y = (tile_ids // TILE_COLS * TILE_SIDE)[:, None] + (pixel_ids // TILE_SIDE)[None, :]
    delta_x = pixel_x.astype(jnp.float32)[:, None, :] + 0.5 - picked[0][:, :, None]
    delta_y = pixel_y.astype(jnp.float32)[:, None, :] + 0.5 - picked[1][:, :, None]
    quadric = (
        picked[2][:, :, None] * delta_x * delta_x
        + 2.0 * picked[3][:, :, None] * delta_x * delta_y
        + picked[4][:, :, None] * delta_y * delta_y
    )
    live_mask = jnp.arange(list_size, dtype=jnp.int32)[None, :] < lengths[:, None]
    alphas = jnp.where(live_mask[:, :, None], picked[5][:, :, None] * jnp.exp(-0.5 * quadric), 0.0)
    log_keep = jnp.log1p(-alphas)
    weight = jnp.exp(jnp.cumsum(log_keep, axis=1) - log_keep) * alphas
    render = jnp.stack(
        [jnp.sum(weight * picked[6 + channel][:, :, None], axis=1) for channel in range(3)], axis=1
    )
    return jnp.sum(jnp.abs(render - target))


def adam_update(params, first_moment, second_moment, gradient):
    new_first = beta_one * first_moment + (1.0 - beta_one) * gradient
    new_second = beta_two * second_moment + (1.0 - beta_two) * gradient * gradient
    step_size = learning * (new_first / (1.0 - beta_one**ADAM_STEP))
    new_params = params - step_size / (
        jnp.sqrt(new_second / (1.0 - beta_two**ADAM_STEP)) + adam_eps
    )
    return (new_params, new_first, new_second)


def select_rows(piece, positions):
    width_here = piece.shape[1]
    inside = (positions >= 0) & (positions < width_here)
    values = jnp.take(piece, jnp.clip(positions, 0, width_here - 1), axis=1)
    return jnp.where(inside[None, :], values, 0.0)


def spread_rows(row_grads, positions, block_rows):
    width_here = block_rows * 128
    inside = (positions >= 0) & (positions < width_here)
    dense_rows = jnp.zeros((row_grads.shape[0], width_here), jnp.float32)
    dense_rows = dense_rows.at[:, jnp.clip(positions, 0, width_here - 1)].add(
        jnp.where(inside[None, :], row_grads, 0.0)
    )
    return dense_rows.reshape(row_grads.shape[0], block_rows, 128).transpose(1, 0, 2)


def per_device(params, first_moment, second_moment, cameras, target, lists, lengths):
    view_count = lax.axis_size("views")
    tile_groups = lax.axis_size("tiles")
    my_view = lax.axis_index("views")
    my_tiles = lax.axis_index("tiles")
    owned = params.shape[1]
    tile_dev = target.shape[1]
    list_size = lists.shape[2]
    width = TILE_COLS * TILE_SIDE
    height = tile_dev * tile_groups // TILE_COLS * TILE_SIDE
    focal_len = float(width)

    def all_views(values):
        return jnp.stack(
            [
                project(values, cameras[camera_at], focal_len, 0.5 * width, 0.5 * height)
                for camera_at in range(view_count)
            ]
        )

    projected, pullback = jax.vjp(all_views, params)
    entries = lists[0].reshape(-1)
    picked = select_rows(
        lax.dynamic_index_in_dim(
            lax.all_gather(projected, ("views", "tiles"), axis=2, tiled=True),
            my_view,
            0,
            keepdims=False,
        ),
        entries,
    )
    per_block = 4
    block_count = tile_dev // per_block
    blocks = (
        picked.reshape(-1, block_count, per_block, list_size).transpose(1, 0, 2, 3),
        lengths[0].reshape(block_count, per_block),
        target[0].reshape(block_count, per_block, 3, -1),
        my_tiles * tile_dev + jnp.arange(block_count, dtype=jnp.int32) * per_block,
    )

    def block_gradient(block):
        chosen, block_len, block_target, first_tile = block
        _, pull_block = jax.vjp(
            lambda inner: composite(inner, block_len, block_target, first_tile), chosen
        )
        return pull_block(jnp.ones((), jnp.float32))[0]

    row_grads = (
        lax.map(block_gradient, blocks).transpose(1, 0, 2, 3).reshape(projected.shape[1], -1)
    )
    selector = (jnp.arange(view_count) == my_view).astype(jnp.float32)
    shares = lax.psum_scatter(
        spread_rows(row_grads, entries, owned // 128 * lax.axis_size(("views", "tiles")))[:, None]
        * selector[None, :, None, None],
        ("views", "tiles"),
        scatter_dimension=0,
        tiled=True,
    )
    owner_grads = shares.transpose(1, 2, 0, 3).reshape(view_count, -1, owned)
    gradient = pullback(owner_grads)[0]
    return adam_update(params, first_moment, second_moment, gradient)


def solution(mesh):
    placed = (
        P(None, ("views", "tiles")),
        P(None, ("views", "tiles")),
        P(None, ("views", "tiles")),
        P(),
        P("views", "tiles", None, None),
        P("views", "tiles", None),
        P("views", "tiles"),
    )
    return jax.shard_map(
        per_device,
        mesh=mesh,
        in_specs=placed,
        out_specs=(
            P(None, ("views", "tiles")),
            P(None, ("views", "tiles")),
            P(None, ("views", "tiles")),
        ),
        check_vma=False,
    )
```

profile of v0, /device:TPU:0, one launch (start us, length us, event | category | flops | bytes accessed | tf_op | source)
XLA Modules:
  0.0 513.2 jit_solution(6132033900119128038)
XLA Ops:
  7.2 1.5 fusion.438
  13.2 2.1 fusion.437
  40.7 1.5 add_add_fusion.78
  53.8 1.5 add_add_fusion.69
  63.2 1.5 add_add_fusion.60
  70.6 3.5 fusion.430
  74.2 3.5 fusion.436
  78.5 3.5 fusion.432
  82.5 3.4 fusion.434
  86.5 48.3 %all_gather.3 = f32[4,9,4096]{2,1,0:T(8,128)S(1)} all-gather(f32[4,9,128]{2,1,0:T(8,128)S(1)} %pad_maximum_fusion), channel_id=1, replica_groups=mesh['views'=4,'tiles'=8] {'views','tiles'}, dimensions={2}, use_global_device_ids=true | all-gather | bytes 608256 | tf_op jit(solution)/shard_map/all_gather | solution.py:245
  135.6 14.4 %gather_fusion = f32[4096,9]{1,0:T(8,128)} fusion(f32[9,4096]{0,1:T(8,128)S(1)} %bitcast.928, s32[4096]{0:T(1024)S(1)} %broadcast_clamp_fusion), kind=kCustom, calls=%fused_computation | custom fusion | bytes 311296 | tf_op jit(solution)/shard_map/jit(_take)/gather | solution.py:207
  150.0 2.2 copy.36
  155.4 147.7 %while.13 = (s32[]{:T(128)}, f32[4,9,4,256]{3,2,1,0:T(4,128)}, s32[4,4]{1,0:T(4,128)}, f32[4,9,4,256]{3,2,1,0:T(4,128)}, s32[4]{0:T(128)}, /*index=5*/f32[4,4,3,...) while((s32[]{:T(128)}, f32[4,9,4,256]{3,2,1,0:T(4,128)}, ...), condition=%wide.region_18.19_spmd, body=%wide.region_1.18_spmd.sunk | while | flops 97887840 | bytes 31174648 | solution.py:269
  159.9 4.4 fusion.450
  164.4 1.5 fusion.451
  166.5 2.8 multiply_reduce_fusion.14
  171.3 12.4 %fusion.452 = f32[4,256,2,128]{1,2,3,0:T(2,128)S(1)} fusion(f32[4,256,2,128]{1,2,3,0:T(2,128)S(1)} %broadcast_add_fusion.12, f32[4,256,2,128]{1,2,3,0:T(2,128)S(1)} %fusion.450, f32[4,2,128]{1,2,0:T(8,128)S(1)} %copy.60, f32[4,256]{1,0:T(4,128)S(1)} %get-tuple-element.1043, f32[4,2,128]{1,2,0:T(8,128)} %copy.61, ...), kind=kOutput, calls=%fused_computation.50.clone.1 | output fusion | flops 35651584 | bytes 3170304 | tf_op jit(solution)/shard_map/reduce-window.18
  184.8 1.7 broadcast_add_fusion.13
  186.6 2.6 multiply_reduce_fusion.15
  189.2 2.4 fusion.453
  196.9 4.4 fusion.450
  201.3 1.5 fusion.451
  203.4 2.8 multiply_reduce_fusion.14
  208.2 12.4 %fusion.452 = f32[4,256,2,128]{1,2,3,0:T(2,128)S(1)} fusion(f32[4,256,2,128]{1,2,3,0:T(2,128)S(1)} %broadcast_add_fusion.12, f32[4,256,2,128]{1,2,3,0:T(2,128)S(1)} %fusion.450, f32[4,2,128]{1,2,0:T(8,128)S(1)} %copy.60, f32[4,256]{1,0:T(4,128)S(1)} %get-tuple-element.1043, f32[4,2,128]{1,2,0:T(8,128)} %copy.61, ...), kind=kOutput, calls=%fused_computation.50.clone.1 | output fusion | flops 35651584 | bytes 3170304 | tf_op jit(solution)/shard_map/reduce-window.18
  221.7 1.7 broadcast_add_fusion.13
  223.5 2.6 multiply_reduce_fusion.15
  226.1 2.4 fusion.453
  233.8 4.4 fusion.450
  238.3 1.5 fusion.451
  240.4 2.8 multiply_reduce_fusion.14
  245.2 12.4 %fusion.452 = f32[4,256,2,128]{1,2,3,0:T(2,128)S(1)} fusion(f32[4,256,2,128]{1,2,3,0:T(2,128)S(1)} %broadcast_add_fusion.12, f32[4,256,2,128]{1,2,3,0:T(2,128)S(1)} %fusion.450, f32[4,2,128]{1,2,0:T(8,128)S(1)} %copy.60, f32[4,256]{1,0:T(4,128)S(1)} %get-tuple-element.1043, f32[4,2,128]{1,2,0:T(8,128)} %copy.61, ...), kind=kOutput, calls=%fused_computation.50.clone.1 | output fusion | flops 35651584 | bytes 3170304 | tf_op jit(solution)/shard_map/reduce-window.18
  258.7 1.7 broadcast_add_fusion.13
  260.5 2.6 multiply_reduce_fusion.15
  263.1 2.4 fusion.453
  270.7 4.4 fusion.450
  275.2 1.5 fusion.451
  277.3 2.8 multiply_reduce_fusion.14
  282.1 12.4 %fusion.452 = f32[4,256,2,128]{1,2,3,0:T(2,128)S(1)} fusion(f32[4,256,2,128]{1,2,3,0:T(2,128)S(1)} %broadcast_add_fusion.12, f32[4,256,2,128]{1,2,3,0:T(2,128)S(1)} %fusion.450, f32[4,2,128]{1,2,0:T(8,128)S(1)} %copy.60, f32[4,256]{1,0:T(4,128)S(1)} %get-tuple-element.1043, f32[4,2,128]{1,2,0:T(8,128)} %copy.61, ...), kind=kOutput, calls=%fused_computation.50.clone.1 | output fusion | flops 35651584 | bytes 3170304 | tf_op jit(solution)/shard_map/reduce-window.18
  295.6 1.7 broadcast_add_fusion.13
  297.4 2.6 multiply_reduce_fusion.15
  300.0 2.4 fusion.453
  303.1 2.8 copy.38
  305.9 3.6 bitcast_select_fusion
  309.5 24.0 %scatter_custom_fusion = f32[9,4096]{0,1:T(8,128)} fusion(s32[4096]{0:T(1024)S(1)} %bitcast.966, f32[9,4096]{0,1:T(8,128)S(1)} %bitcast_select_fusion, f32[]{:T(128)} %constant.226.clone.1), kind=kCustom, calls=%fused_computation.120 | custom fusion | flops 36864 | bytes 2244612 | tf_op jit(solution)/shard_map/scatter-add | solution.py:215
  333.7 2.2 copy.39
  336.1 1.8 broadcast_multiply_fusion
  337.9 131.1 %reduce-scatter.2.cloned.1.call-done = f32[1,4,9,128]{3,2,1,0:T(8,128)} async-done(((f32[32,4,9,128]{3,2,1,0:T(8,128)}), f32[1,4,9,128]{3,2,1,0:T(8,128)}) %reduce-scatter.2.cloned.1.call-update) | async-done | bytes 18448 | tf_op jit(solution)/shard_map/reduce_scatter | solution.py:272
  504.1 2.3 divide_subtract_fusion
  (535 shorter events, 90.3 us)
Async XLA Ops:
  7.2 461.9 %reduce-scatter.2.cloned.1.call-start = ((), (), s32[]{:S(2)}) async-start(), calls=%async_computation.1 | async-start | bytes 1081344 | tf_op jit(solution)/shard_map/reduce_scatter | solution.py:272
  74.2 61.3 %copy-start.111 = (f32[1,128]{1,0:T(1,128)}, f32[1,128]{1,0:T(1,128)S(1)}, u32[]{:S(2)}) copy-start(f32[1,128]{1,0:T(1,128)S(1)} %get-tuple-element.324) | copy-start | bytes 1540
  77.8 57.7 %copy-start.113 = (f32[1,128]{1,0:T(1,128)}, f32[1,128]{1,0:T(1,128)S(1)}, u32[]{:S(2)}) copy-start(f32[1,128]{1,0:T(1,128)S(1)} %get-tuple-element.483) | copy-start | bytes 1540
  82.1 53.4 %copy-start.112 = (f32[1,128]{1,0:T(1,128)}, f32[1,128]{1,0:T(1,128)S(1)}, u32[]{:S(2)}) copy-start(f32[1,128]{1,0:T(1,128)S(1)} %get-tuple-element.383) | copy-start | bytes 1540
  86.0 49.6 %copy-start.114 = (f32[1,128]{1,0:T(1,128)}, f32[1,128]{1,0:T(1,128)S(1)}, u32[]{:S(2)}) copy-start(f32[1,128]{1,0:T(1,128)S(1)} %get-tuple-element.433) | copy-start | bytes 1540
  86.0 49.6 %copy-start.118 = (f32[1,128]{1,0:T(1,128)}, f32[1,128]{1,0:T(1,128)S(1)}, u32[]{:S(2)}) copy-start(f32[1,128]{1,0:T(1,128)S(1)} %get-tuple-element.435) | copy-start | bytes 1540
  135.6 17.2 %copy-start.3 = (f32[1,16,3,256]{3,1,2,0:T(8,128)S(1)}, f32[1,16,3,256]{3,1,2,0:T(8,128)}, u32[]{:S(2)}) copy-start(f32[1,16,3,256]{3,1,2,0:T(8,128)} %param.14) | copy-start | bytes 147460
  135.6 17.7 %copy-start.120 = (s32[1,16]{1,0:T(1,128)S(1)}, s32[1,16]{1,0:T(1,128)}, u32[]{:S(2)}) copy-start(s32[1,16]{1,0:T(1,128)} %param.16) | copy-start | bytes 196
  333.5 135.5 %copy-start.41 = (f32[1,128]{1,0:T(1,128)S(1)}, f32[1,128]{1,0:T(1,128)}, u32[]{:S(2)}) copy-start(f32[1,128]{1,0:T(1,128)} %copy-done.40) | copy-start | bytes 1540
  333.5 135.5 %copy-start.43 = (f32[1,128]{1,0:T(1,128)S(1)}, f32[1,128]{1,0:T(1,128)}, u32[]{:S(2)}) copy-start(f32[1,128]{1,0:T(1,128)} %copy-done.42) | copy-start | bytes 1540
  333.5 135.5 %copy-start.45 = (f32[1,128]{1,0:T(1,128)S(1)}, f32[1,128]{1,0:T(1,128)}, u32[]{:S(2)}) copy-start(f32[1,128]{1,0:T(1,128)} %copy-done.44) | copy-start | bytes 1540
  333.5 136.3 %copy-start.35 = (f32[1,128]{1,0:T(1,128)S(1)}, f32[1,128]{1,0:T(1,128)}, u32[]{:S(2)}) copy-start(f32[1,128]{1,0:T(1,128)} %copy-done.34) | copy-start | bytes 1540
  333.5 136.3 %copy-start.37 = (f32[1,128]{1,0:T(1,128)S(1)}, f32[1,128]{1,0:T(1,128)}, u32[]{:S(2)}) copy-start(f32[1,128]{1,0:T(1,128)} %copy-done.36) | copy-start | bytes 1540
  333.5 136.3 %copy-start.39 = (f32[1,128]{1,0:T(1,128)S(1)}, f32[1,128]{1,0:T(1,128)}, u32[]{:S(2)}) copy-start(f32[1,128]{1,0:T(1,128)} %copy-done.38) | copy-start | bytes 1540
  333.6 136.3 %copy-start.53 = (f32[1,128]{1,0:T(1,128)S(1)}, f32[1,128]{1,0:T(1,128)}, u32[]{:S(2)}) copy-start(f32[1,128]{1,0:T(1,128)} %copy-done.52) | copy-start | bytes 1540
  333.6 136.3 %copy-start.55 = (f32[1,128]{1,0:T(1,128)S(1)}, f32[1,128]{1,0:T(1,128)}, u32[]{:S(2)}) copy-start(f32[1,128]{1,0:T(1,128)} %copy-done.54) | copy-start | bytes 1540
  333.6 136.3 %copy-start.57 = (f32[1,128]{1,0:T(1,128)S(1)}, f32[1,128]{1,0:T(1,128)}, u32[]{:S(2)}) copy-start(f32[1,128]{1,0:T(1,128)} %copy-done.56) | copy-start | bytes 1540
  333.6 137.1 %copy-start.47 = (f32[1,128]{1,0:T(1,128)S(1)}, f32[1,128]{1,0:T(1,128)}, u32[]{:S(2)}) copy-start(f32[1,128]{1,0:T(1,128)} %copy-done.46) | copy-start | bytes 1540
  333.6 137.1 %copy-start.49 = (f32[1,128]{1,0:T(1,128)S(1)}, f32[1,128]{1,0:T(1,128)}, u32[]{:S(2)}) copy-start(f32[1,128]{1,0:T(1,128)} %copy-done.48) | copy-start | bytes 1540
  333.6 137.1 %copy-start.51 = (f32[1,128]{1,0:T(1,128)S(1)}, f32[1,128]{1,0:T(1,128)}, u32[]{:S(2)}) copy-start(f32[1,128]{1,0:T(1,128)} %copy-done.50) | copy-start | bytes 1540
  333.6 138.0 %copy-start.8 = (f32[1,128]{1,0:T(1,128)S(1)}, f32[1,128]{1,0:T(1,128)}, u32[]{:S(2)}) copy-start(f32[1,128]{1,0:T(1,128)} %get-tuple-element.337) | copy-start | bytes 1540
  333.6 138.8 %copy-start.9 = (f32[1,128]{1,0:T(1,128)S(1)}, f32[1,128]{1,0:T(1,128)}, u32[]{:S(2)}) copy-start(f32[1,128]{1,0:T(1,128)} %get-tuple-element.386) | copy-start | bytes 1540
  333.6 141.1 %copy-start.11 = (f32[1,128]{1,0:T(1,128)S(1)}, f32[1,128]{1,0:T(1,128)}, u32[]{:S(2)}) copy-start(f32[1,128]{1,0:T(1,128)} %get-tuple-element.436) | copy-start | bytes 1540
  333.6 142.8 %copy-start.10 = (f32[1,128]{1,0:T(1,128)S(1)}, f32[1,128]{1,0:T(1,128)}, u32[]{:S(2)}) copy-start(f32[1,128]{1,0:T(1,128)} %get-tuple-element.486) | copy-start | bytes 1540
  333.7 142.9 %copy-start.2 = (f32[59,128]{1,0:T(8,128)S(1)}, f32[59,128]{1,0:T(8,128)}, u32[]{:S(2)}) copy-start(f32[59,128]{1,0:T(8,128)} %param.10) | copy-start | bytes 90628
  335.9 148.8 %copy-start.23 = (f32[1,128]{1,0:T(1,128)S(1)}, f32[1,128]{1,0:T(1,128)}, u32[]{:S(2)}) copy-start(f32[1,128]{1,0:T(1,128)} %copy-done.22) | copy-start | bytes 1540
  335.9 148.8 %copy-start.25 = (f32[1,128]{1,0:T(1,128)S(1)}, f32[1,128]{1,0:T(1,128)}, u32[]{:S(2)}) copy-start(f32[1,128]{1,0:T(1,128)} %copy-done.24) | copy-start | bytes 1540
  335.9 148.8 %copy-start.29 = (f32[1,128]{1,0:T(1,128)S(1)}, f32[1,128]{1,0:T(1,128)}, u32[]{:S(2)}) copy-start(f32[1,128]{1,0:T(1,128)} %copy-done.28) | copy-start | bytes 1540
  335.9 150.5 %copy-start.19 = (f32[1,128]{1,0:T(1,128)S(1)}, f32[1,128]{1,0:T(1,128)}, u32[]{:S(2)}) copy-start(f32[1,128]{1,0:T(1,128)} %copy-done.18) | copy-start | bytes 1540
  335.9 150.5 %copy-start.21 = (f32[1,128]{1,0:T(1,128)S(1)}, f32[1,128]{1,0:T(1,128)}, u32[]{:S(2)}) copy-start(f32[1,128]{1,0:T(1,128)} %copy-done.20) | copy-start | bytes 1540
  335.9 150.5 %copy-start.27 = (f32[1,128]{1,0:T(1,128)S(1)}, f32[1,128]{1,0:T(1,128)}, u32[]{:S(2)}) copy-start(f32[1,128]{1,0:T(1,128)} %copy-done.26) | copy-start | bytes 1540
  335.9 152.1 %copy-start.17 = (f32[1,128]{1,0:T(1,128)S(1)}, f32[1,128]{1,0:T(1,128)}, u32[]{:S(2)}) copy-start(f32[1,128]{1,0:T(1,128)} %copy-done.16) | copy-start | bytes 1540
  335.9 152.1 %copy-start.31 = (f32[1,128]{1,0:T(1,128)S(1)}, f32[1,128]{1,0:T(1,128)}, u32[]{:S(2)}) copy-start(f32[1,128]{1,0:T(1,128)} %copy-done.30) | copy-start | bytes 1540
  336.0 152.1 %copy-start.33 = (f32[1,128]{1,0:T(1,128)S(1)}, f32[1,128]{1,0:T(1,128)}, u32[]{:S(2)}) copy-start(f32[1,128]{1,0:T(1,128)} %copy-done.32) | copy-start | bytes 1540
  336.0 153.8 %copy-start.7 = (f32[1,128]{1,0:T(1,128)S(1)}, f32[1,128]{1,0:T(1,128)}, u32[]{:S(2)}) copy-start(f32[1,128]{1,0:T(1,128)} %copy-done.6) | copy-start | bytes 1540
  336.0 153.8 %copy-start.13 = (f32[1,128]{1,0:T(1,128)S(1)}, f32[1,128]{1,0:T(1,128)}, u32[]{:S(2)}) copy-start(f32[1,128]{1,0:T(1,128)} %copy-done.12) | copy-start | bytes 1540
  336.0 153.8 %copy-start.15 = (f32[1,128]{1,0:T(1,128)S(1)}, f32[1,128]{1,0:T(1,128)}, u32[]{:S(2)}) copy-start(f32[1,128]{1,0:T(1,128)} %copy-done.14) | copy-start | bytes 1540
  336.0 161.0 %copy-start.75 = (f32[1,128]{1,0:T(1,128)S(1)}, f32[1,128]{1,0:T(1,128)}, u32[]{:S(2)}) copy-start(f32[1,128]{1,0:T(1,128)} %copy-done.74) | copy-start | bytes 1540
  336.0 161.7 %copy-start.73 = (f32[1,128]{1,0:T(1,128)S(1)}, f32[1,128]{1,0:T(1,128)}, u32[]{:S(2)}) copy-start(f32[1,128]{1,0:T(1,128)} %copy-done.72) | copy-start | bytes 1540
  336.0 162.5 %copy-start.71 = (f32[1,128]{1,0:T(1,128)S(1)}, f32[1,128]{1,0:T(1,128)}, u32[]{:S(2)}) copy-start(f32[1,128]{1,0:T(1,128)} %copy-done.70) | copy-start | bytes 1540
  336.0 163.3 %copy-start.69 = (f32[1,128]{1,0:T(1,128)S(1)}, f32[1,128]{1,0:T(1,128)}, u32[]{:S(2)}) copy-start(f32[1,128]{1,0:T(1,128)} %copy-done.68) | copy-start | bytes 1540
  336.0 164.1 %copy-start.67 = (f32[1,128]{1,0:T(1,128)S(1)}, f32[1,128]{1,0:T(1,128)}, u32[]{:S(2)}) copy-start(f32[1,128]{1,0:T(1,128)} %copy-done.66) | copy-start | bytes 1540
  336.0 164.8 %copy-start.65 = (f32[1,128]{1,0:T(1,128)S(1)}, f32[1,128]{1,0:T(1,128)}, u32[]{:S(2)}) copy-start(f32[1,128]{1,0:T(1,128)} %copy-done.64) | copy-start | bytes 1540
  336.1 165.6 %copy-start.63 = (f32[1,128]{1,0:T(1,128)S(1)}, f32[1,128]{1,0:T(1,128)}, u32[]{:S(2)}) copy-start(f32[1,128]{1,0:T(1,128)} %copy-done.62) | copy-start | bytes 1540
  336.1 166.4 %copy-start.59 = (f32[1,128]{1,0:T(1,128)S(1)}, f32[1,128]{1,0:T(1,128)}, u32[]{:S(2)}) copy-start(f32[1,128]{1,0:T(1,128)} %copy-done.58) | copy-start | bytes 1540
  336.1 166.4 %copy-start.61 = (f32[1,128]{1,0:T(1,128)S(1)}, f32[1,128]{1,0:T(1,128)}, u32[]{:S(2)}) copy-start(f32[1,128]{1,0:T(1,128)} %copy-done.60) | copy-start | bytes 1540
  336.1 168.0 %copy-start.4 = (f32[59,128]{1,0:T(8,128)S(1)}, f32[59,128]{1,0:T(8,128)}, u32[]{:S(2)}) copy-start(f32[59,128]{1,0:T(8,128)} %param.11) | copy-start | bytes 90628
  336.1 168.0 %copy-start.5 = (f32[59,128]{1,0:T(8,128)S(1)}, f32[59,128]{1,0:T(8,128)}, u32[]{:S(2)}) copy-start(f32[59,128]{1,0:T(8,128)} %param.12) | copy-start | bytes 90628
  (80 other events, 175.5 us)
Sparse Core Ops, SparseCore 0:
  338.1 130.9 reduce-scatter.1
where the time goes:
time: 517 us; the launch traced here: 513 us
  other arithmetic  222 us (43%)
  waiting for transfers between devices  131 us (25%)
  between operations  55.8 us (11%)
  local copies, waits for them, and re-layouts  54.7 us (11%)
  blocking collectives  48.3 us (9%)
    reduce_scatter x1, waiting for transfers between devices, per_device(): lax.psum_scatter(spread_rows(row_grads, entries, owned // 128 * lax.axis_...  131 us
    another operation x24, other arithmetic  64.2 us
    all_gather x1, blocking collectives, per_device(): lax.all_gather(projected, ('views', 'tiles'), axis=2, tiled=True)  48.3 us
    scatter-add x1, other arithmetic, spread_rows(): dense_rows.at[:, jnp.clip(positions, 0, width_here - 1)]  24 us
    select_n x4, other arithmetic, composite(): jnp.where(live_mask[:, :, None], picked[5][:, :, None] * jnp.exp(-0.5 * q...  17.7 us
    gather x2, local copies, waits for them, and re-layouts, select_rows(): values = jnp.take(piece, jnp.clip(positions, 0, width_here - 1), axis=1)  16.6 us
    div x4, other arithmetic, project(): cov_a / determinant  14 us
    add x12, other arithmetic, project(): 0.5 + sum((basis[coef_at] * params[11 + 3 * coef_at + channel] for coef_a...  12.9 us
  transfers between devices with their start and end apart: 1, of which 1 were waited for; matrix products, arithmetic and copies ran while one was open for 0% of the time, Pallas kernels for 0%

commit v1 on v0

v1 whole, which is shorter than its diff:
```python
import jax
import jax.numpy as jnp
import numpy as np
from jax import lax
from jax.experimental import pallas as pl
from jax.experimental.pallas import tpu as pltpu
from jax.sharding import PartitionSpec as P

TILE_SIDE = 16
TILE_COLS = 32
ADAM_STEP = 1000


sh_zero = 0.28209479177387814
sh_first = 0.4886025119029199
sh_second = (
    1.0925484305920792,
    -1.0925484305920792,
    0.31539156525252005,
    -1.0925484305920792,
    0.5462742152960396,
)
sh_third = (
    -0.5900435899266435,
    2.890611442640554,
    -0.4570457994644658,
    0.3731763325901154,
    -0.4570457994644658,
    1.445305721320277,
    -0.5900435899266435,
)
beta_one = 0.9
beta_two = 0.999
adam_eps = 1e-15
learning = np.concatenate(
    [
        np.full(3, 0.00016),
        np.full(3, 0.005),
        np.full(4, 0.001),
        np.full(1, 0.05),
        np.full(3, 0.0025),
        np.full(45, 0.000125),
    ]
).astype(np.float32)[:, None]


def matmul_three(left, right):
    return [
        [
            left[row_at][0] * right[0][col_at]
            + left[row_at][1] * right[1][col_at]
            + left[row_at][2] * right[2][col_at]
            for col_at in range(3)
        ]
        for row_at in range(3)
    ]


def camera_rotation(camera):
    cos_a, sin_a = (jnp.cos(camera[0]), jnp.sin(camera[0]))
    cos_b, sin_b = (jnp.cos(camera[1]), jnp.sin(camera[1]))
    cos_c, sin_c = (jnp.cos(camera[2]), jnp.sin(camera[2]))
    around_x = [[1.0, 0.0, 0.0], [0.0, cos_a, -sin_a], [0.0, sin_a, cos_a]]
    around_y = [[cos_b, 0.0, sin_b], [0.0, 1.0, 0.0], [-sin_b, 0.0, cos_b]]
    around_z = [[cos_c, -sin_c, 0.0], [sin_c, cos_c, 0.0], [0.0, 0.0, 1.0]]
    return matmul_three(around_z, matmul_three(around_y, around_x))


def sh_basis(along_x, along_y, along_z):
    square_x, square_y, square_z = (along_x * along_x, along_y * along_y, along_z * along_z)
    both_xy, both_yz, both_xz = (along_x * along_y, along_y * along_z, along_x * along_z)
    return [
        sh_zero + 0.0 * along_x,
        -sh_first * along_y,
        sh_first * along_z,
        -sh_first * along_x,
        sh_second[0] * both_xy,
        sh_second[1] * both_yz,
        sh_second[2] * (2.0 * square_z - square_x - square_y),
        sh_second[3] * both_xz,
        sh_second[4] * (square_x - square_y),
        sh_third[0] * along_y * (3.0 * square_x - square_y),
        sh_third[1] * both_xy * along_z,
        sh_third[2] * along_y * (4.0 * square_z - square_x - square_y),
        sh_third[3] * along_z * (2.0 * square_z - 3.0 * square_x - 3.0 * square_y),
        sh_third[4] * along_x * (4.0 * square_z - square_x - square_y),
        sh_third[5] * along_z * (square_x - square_y),
        sh_third[6] * along_x * (square_x - 3.0 * square_y),
    ]


def project(rows, camera, focal_len, center_x, center_y):
    rotation = camera_rotation(camera)
    means = rows[0:3]
    point = [
        rotation[axis_at][0] * means[0]
        + rotation[axis_at][1] * means[1]
        + rotation[axis_at][2] * means[2]
        + camera[3 + axis_at]
        for axis_at in range(3)
    ]
    inverse_z = 1.0 / point[2]
    screen_u = focal_len * point[0] * inverse_z + center_x
    screen_v = focal_len * point[1] * inverse_z + center_y
    scales = [jnp.exp(value) for value in rows[3:6]]
    norm = rows[6] * rows[6] + rows[7] * rows[7] + rows[8] * rows[8] + rows[9] * rows[9]
    inverse_norm = lax.rsqrt(norm)
    real_part, imag_x, imag_y, imag_z = [value * inverse_norm for value in rows[6:10]]
    spin = [
        [
            1.0 - 2.0 * (imag_y * imag_y + imag_z * imag_z),
            2.0 * (imag_x * imag_y - real_part * imag_z),
            2.0 * (imag_x * imag_z + real_part * imag_y),
        ],
        [
            2.0 * (imag_x * imag_y + real_part * imag_z),
            1.0 - 2.0 * (imag_x * imag_x + imag_z * imag_z),
            2.0 * (imag_y * imag_z - real_part * imag_x),
        ],
        [
            2.0 * (imag_x * imag_z - real_part * imag_y),
            2.0 * (imag_y * imag_z + real_part * imag_x),
            1.0 - 2.0 * (imag_x * imag_x + imag_y * imag_y),
        ],
    ]
    turned = matmul_three(rotation, spin)
    shaped = [
        [turned[row_at][col_at] * scales[col_at] for col_at in range(3)] for row_at in range(3)
    ]
    near_x = [
        focal_len * inverse_z * shaped[0][col_at]
        - focal_len * point[0] * inverse_z * inverse_z * shaped[2][col_at]
        for col_at in range(3)
    ]
    near_y = [
        focal_len * inverse_z * shaped[1][col_at]
        - focal_len * point[1] * inverse_z * inverse_z * shaped[2][col_at]
        for col_at in range(3)
    ]
    cov_a = near_x[0] * near_x[0] + near_x[1] * near_x[1] + near_x[2] * near_x[2] + 0.3
    cov_b = near_x[0] * near_y[0] + near_x[1] * near_y[1] + near_x[2] * near_y[2]
    cov_c = near_y[0] * near_y[0] + near_y[1] * near_y[1] + near_y[2] * near_y[2] + 0.3
    determinant = cov_a * cov_c - cov_b * cov_b
    offset = [
        means[axis_at]
        + rotation[0][axis_at] * camera[3]
        + rotation[1][axis_at] * camera[4]
        + rotation[2][axis_at] * camera[5]
        for axis_at in range(3)
    ]
    inverse_len = lax.rsqrt(offset[0] * offset[0] + offset[1] * offset[1] + offset[2] * offset[2])
    basis = sh_basis(offset[0] * inverse_len, offset[1] * inverse_len, offset[2] * inverse_len)
    colors = [
        0.5 + sum((basis[coef_at] * rows[11 + 3 * coef_at + channel] for coef_at in range(16)))
        for channel in range(3)
    ]
    return (
        screen_u,
        screen_v,
        cov_c / determinant,
        -cov_b / determinant,
        cov_a / determinant,
        colors[0],
        colors[1],
        colors[2],
    )


def exchange(source_of, landing_ref, send_sem, recv_sem, peers, tile_groups, me):
    def copy_to(step):
        peer = lax.rem(me + step, peers)
        return pltpu.make_async_remote_copy(
            src_ref=source_of(peer),
            dst_ref=landing_ref.at[me],
            send_sem=send_sem.at[step],
            recv_sem=recv_sem.at[step],
            device_id=(peer // tile_groups, lax.rem(peer, tile_groups)),
            device_id_type=pl.DeviceIdType.MESH,
        )

    def start(step, carry):
        copy_to(step).start()
        return carry

    def finish(step, carry):
        copy_to(step).wait()
        return carry

    return (
        lambda: lax.fori_loop(1, peers, start, 0),
        lambda: lax.fori_loop(1, peers, finish, 0),
    )


def greet(peers, tile_groups, me):
    barrier = pltpu.get_barrier_semaphore()

    def one(step, carry):
        peer = lax.rem(me + step, peers)
        pl.semaphore_signal(
            barrier,
            inc=1,
            device_id=(peer // tile_groups, lax.rem(peer, tile_groups)),
            device_id_type=pl.DeviceIdType.MESH,
        )
        return carry

    lax.fori_loop(1, peers, one, 0)
    return lambda: pl.semaphore_wait(barrier, peers - 1)


def camera_columns(cameras_ref):
    return [cameras_ref[:, at : at + 1] for at in range(6)]


def sigmoid(value):
    return 1.0 / (1.0 + jnp.exp(-value))


def project_kernel(
    peers, tile_groups, width, height, cameras_ref, params_ref, table_ref, rows_ref, send_sem, recv_sem
):
    my_view = lax.axis_index("views")
    me = my_view * tile_groups + lax.axis_index("tiles")
    everyone_here = greet(peers, tile_groups, me)
    view_count = rows_ref.shape[0]
    owned = params_ref.shape[1]
    values = [params_ref[at : at + 1, :] for at in range(59)]
    made = project(
        values, camera_columns(cameras_ref), float(width), 0.5 * width, 0.5 * height
    )
    opacity = jnp.broadcast_to(sigmoid(values[10]), (view_count, owned))
    for row_at, value in enumerate(made[:5] + (opacity,) + made[5:]):
        rows_ref[:, row_at, :] = value
    everyone_here()
    start, finish = exchange(
        lambda peer: rows_ref.at[peer // tile_groups],
        table_ref,
        send_sem,
        recv_sem,
        peers,
        tile_groups,
        me,
    )
    start()
    table_ref[pl.ds(me, 1)] = rows_ref[pl.ds(my_view, 1)]
    finish()


def collect_kernel(peers, tile_groups, dense_ref, out_ref, landing_ref, send_sem, recv_sem):
    me = lax.axis_index("views") * tile_groups + lax.axis_index("tiles")
    everyone_here = greet(peers, tile_groups, me)
    everyone_here()
    start, finish = exchange(
        lambda peer: dense_ref.at[peer], landing_ref, send_sem, recv_sem, peers, tile_groups, me
    )
    start()
    landing_ref[pl.ds(me, 1)] = dense_ref[pl.ds(me, 1)]
    finish()
    for view_at in range(out_ref.shape[0]):
        out_ref[view_at] = jnp.sum(
            landing_ref[view_at * tile_groups : (view_at + 1) * tile_groups], axis=0
        )


def fold(value):
    return value[0:8] + value[8:16]


def composite_kernel(
    first_tile_ref,
    lengths_ref,
    lists_ref,
    target_ref,
    table_ref,
    dense_ref,
    picked,
    keeps,
    suffix,
    before,
    after,
    alpha_s,
    ratio_s,
    flow_s,
    chosen,
    spread,
):
    f32, bf16 = jnp.float32, jnp.bfloat16
    tile_dev, list_size = lists_ref.shape
    peers, _, owned = table_ref.shape
    per_owner = owned // 128
    halves = list_size // 128
    entries = lists_ref[...]
    block_of = entries >> 7
    column_of = entries & 127

    def gather_from(owner, carry):
        carry = list(carry)
        for part in range(per_owner):
            lanes = slice(part * 128, part * 128 + 128)
            for half in range(halves):
                here = slice(half * 128, half * 128 + 128)
                mask = block_of[:, here] == owner * per_owner + part
                column = column_of[:, here]
                for row_at in range(9):
                    line = table_ref[owner, row_at : row_at + 1, lanes]
                    got = jnp.take_along_axis(
                        jnp.broadcast_to(line, (tile_dev, 128)),
                        column,
                        axis=1,
                        mode="promise_in_bounds",
                    )
                    slot = half * 9 + row_at
                    carry[slot] = jnp.where(mask, got, carry[slot])
        return tuple(carry)

    zeros = tuple(jnp.zeros((tile_dev, 128), f32) for _ in range(halves * 9))
    gathered = lax.fori_loop(0, peers, gather_from, zeros)
    for half in range(halves):
        for row_at in range(9):
            picked[row_at, :, half * 128 : half * 128 + 128] = gathered[half * 9 + row_at]

    row_ids = lax.broadcasted_iota(jnp.int32, (list_size, list_size), 0)
    col_ids = lax.broadcasted_iota(jnp.int32, (list_size, list_size), 1)
    for piece in range(3):
        before[piece * list_size : (piece + 1) * list_size, :] = (row_ids < col_ids).astype(f32).astype(bf16)
    for piece in range(2):
        after[piece * list_size : (piece + 1) * list_size, :] = (row_ids > col_ids).astype(f32).astype(bf16)
    spread[...] = jnp.zeros_like(spread)
    lane_ids = lax.broadcasted_iota(jnp.int32, (1, list_size), 1)
    pixel_ids = lax.broadcasted_iota(jnp.int32, (16, list_size), 0).astype(f32)
    column_ids = lax.broadcasted_iota(jnp.int32, (128, list_size), 0)
    first_tile = first_tile_ref[0]
    group = spread.shape[1] // 32

    def one_tile(tile_at, carry):
        tile_id = first_tile + tile_at
        left = (tile_id % TILE_COLS * TILE_SIDE).astype(f32) + 0.5
        top = (tile_id // TILE_COLS * TILE_SIDE).astype(f32) + 0.5
        u, v, con_a, con_b, con_c, opacity, red, green, blue = [
            picked[row_at, pl.ds(tile_at, 1), :] for row_at in range(9)
        ]
        opacity = jnp.where(lane_ids < lengths_ref[tile_at], opacity, 0.0)
        delta_x = (pixel_ids + left) - u
        part_a = (-0.5 * con_a) * delta_x * delta_x
        part_b = -con_b * delta_x
        half_c = -0.5 * con_c
        deltas_y = [(top + float(line)) - v for line in range(TILE_SIDE)]
        for line in range(TILE_SIDE):
            here = slice(line * 16, line * 16 + 16)
            delta_y = deltas_y[line]
            alphas = opacity * jnp.exp(part_a + delta_y * (part_b + half_c * delta_y))
            log_keep = jnp.log(1.0 - alphas)
            high = log_keep.astype(bf16)
            rest = log_keep - high.astype(f32)
            middle = rest.astype(bf16)
            low = (rest - middle.astype(f32)).astype(bf16)
            keeps[here, 0:list_size] = high
            keeps[here, list_size : 2 * list_size] = middle
            keeps[here, 2 * list_size : 3 * list_size] = low
            alpha_s[here, :] = alphas
            ratio_s[here, :] = alphas * jnp.exp(-log_keep)
        passed = jnp.dot(keeps[...], before[...], preferred_element_type=f32)
        wanted = jnp.concatenate(
            [target_ref[tile_at], jnp.zeros((5, TILE_SIDE * TILE_SIDE), f32)], axis=0
        ).T
        color_sums = [jnp.zeros((8, list_size), f32) for _ in range(3)]
        for line in range(TILE_SIDE):
            here = slice(line * 16, line * 16 + 16)
            weight = jnp.exp(passed[here]) * alpha_s[here, :]
            signs = []
            for channel, color in enumerate((red, green, blue)):
                gap = jnp.sum(weight * color, axis=1, keepdims=True) - wanted[here, channel : channel + 1]
                sign = jnp.where(gap > 0.0, 1.0, jnp.where(gap < 0.0, -1.0, 0.0))
                signs.append(sign)
                color_sums[channel] = color_sums[channel] + fold(weight * sign)
            flow = weight * (signs[0] * red + signs[1] * green + signs[2] * blue)
            high = flow.astype(bf16)
            suffix[here, 0:list_size] = high
            suffix[here, list_size : 2 * list_size] = (flow - high.astype(f32)).astype(bf16)
            flow_s[here, :] = flow
        behind = jnp.dot(suffix[...], after[...], preferred_element_type=f32)
        sums = [jnp.zeros((8, list_size), f32) for _ in range(6)]
        for line in range(TILE_SIDE):
            here = slice(line * 16, line * 16 + 16)
            delta_y = deltas_y[line]
            pull = flow_s[here, :] - behind[here] * ratio_s[here, :]
            pull_x = pull * delta_x
            pull_xx = fold(pull_x * delta_x)
            pull_x = fold(pull_x)
            pull = fold(pull)
            pull_y = pull * delta_y
            terms = (pull, pull_x, pull_y, pull_xx, pull_x * delta_y, pull_y * delta_y)
            sums = [total + term for total, term in zip(sums, terms)]
        flat, by_x, by_y, by_xx, by_xy, by_yy = [
            jnp.sum(total, axis=0, keepdims=True) for total in sums
        ]
        grads = jnp.concatenate(
            [
                con_a * by_x + con_b * by_y,
                con_b * by_x + con_c * by_y,
                -0.5 * by_xx,
                -by_xy,
                -0.5 * by_yy,
                flat,
            ]
            + [jnp.sum(total, axis=0, keepdims=True) for total in color_sums]
            + [jnp.zeros((7, list_size), f32)],
            axis=0,
        )
        high = grads.astype(bf16).astype(f32)
        pieces = jnp.concatenate([high, grads - high], axis=0)
        ids = lists_ref[pl.ds(tile_at, 1), :]
        owner = ids >> 7
        one_hot = (column_ids == (ids & 127)).astype(f32).astype(bf16)

        def spread_group(group_at, carry):
            for at in range(group):
                mask = owner == group_at * group + at
                chosen[at * 32 : at * 32 + 32, :] = jnp.where(mask, pieces, 0.0).astype(bf16)
            spread[group_at] += lax.dot_general(
                chosen[...], one_hot, (((1,), (1,)), ((), ())), preferred_element_type=f32
            )
            return carry

        if spread.shape[0] == 1:
            spread_group(0, 0)
        else:
            lax.fori_loop(0, spread.shape[0], spread_group, 0)
        return carry

    lax.fori_loop(0, tile_dev, one_tile, 0)

    owners_here = group // per_owner

    def finish_group(group_at, carry):
        for at in range(group):
            both = spread[group_at, at * 32 : at * 32 + 32, :]
            lanes = at % per_owner * 128
            dense_ref[group_at * owners_here + at // per_owner, :, lanes : lanes + 128] = (
                both[0:9] + both[16:25]
            )
        return carry

    lax.fori_loop(0, spread.shape[0], finish_group, 0)


def update_kernel(
    width,
    height,
    cameras_ref,
    rates_ref,
    grads_ref,
    params_ref,
    first_ref,
    second_ref,
    new_params_ref,
    new_first_ref,
    new_second_ref,
):
    camera = camera_columns(cameras_ref)
    values = [params_ref[at : at + 1, :] for at in range(59)]
    _, pullback = jax.vjp(
        lambda rows: project(rows, camera, float(width), 0.5 * width, 0.5 * height), values
    )
    given = [grads_ref[:, row_at, :] for row_at in range(9)]
    grads = list(pullback(tuple(given[:5] + given[6:]))[0])
    grads[10] = jnp.sum(given[5], axis=0, keepdims=True) * (1.0 - sigmoid(values[10]))
    for at in range(59):
        new_first_ref[at : at + 1, :] = grads[at]
    gradient = new_first_ref[...]
    new_first = beta_one * first_ref[...] + (1.0 - beta_one) * gradient
    new_second = beta_two * second_ref[...] + (1.0 - beta_two) * gradient * gradient
    new_first_ref[...] = new_first
    new_second_ref[...] = new_second
    step_size = rates_ref[...] * (new_first / (1.0 - beta_one**ADAM_STEP))
    new_params_ref[...] = params_ref[...] - step_size / (
        jnp.sqrt(new_second / (1.0 - beta_two**ADAM_STEP)) + adam_eps
    )


def in_vmem(count):
    return [pl.BlockSpec(memory_space=pltpu.VMEM)] * count


def per_device(params, first_moment, second_moment, cameras, target, lists, lengths):
    f32, bf16 = jnp.float32, jnp.bfloat16
    view_count = lax.axis_size("views")
    tile_groups = lax.axis_size("tiles")
    peers = view_count * tile_groups
    owned = params.shape[1]
    tile_dev = target.shape[1]
    list_size = lists.shape[2]
    pixels = target.shape[3]
    width = TILE_COLS * TILE_SIDE
    height = tile_dev * tile_groups // TILE_COLS * TILE_SIDE
    limit = 56 * 1024 * 1024

    table = pl.pallas_call(
        lambda *refs: project_kernel(peers, tile_groups, width, height, *refs),
        out_shape=jax.ShapeDtypeStruct((peers, 9, owned), f32),
        in_specs=in_vmem(2),
        out_specs=pl.BlockSpec(memory_space=pltpu.VMEM),
        scratch_shapes=[
            pltpu.VMEM((view_count, 9, owned), f32),
            pltpu.SemaphoreType.DMA((peers,)),
            pltpu.SemaphoreType.DMA((peers,)),
        ],
        compiler_params=pltpu.CompilerParams(
            collective_id=0, has_side_effects=True, vmem_limit_bytes=limit
        ),
        name="project_rows",
    )(cameras, params)

    blocks = peers * owned // 128
    group = 32
    first_tile = (lax.axis_index("tiles") * tile_dev).astype(jnp.int32).reshape(1)
    dense = pl.pallas_call(
        composite_kernel,
        out_shape=jax.ShapeDtypeStruct((peers, 9, owned), f32),
        in_specs=[pl.BlockSpec(memory_space=pltpu.SMEM)] * 2 + in_vmem(3),
        out_specs=pl.BlockSpec(memory_space=pltpu.VMEM),
        scratch_shapes=[
            pltpu.VMEM((9, tile_dev, list_size), f32),
            pltpu.VMEM((pixels, 3 * list_size), bf16),
            pltpu.VMEM((pixels, 2 * list_size), bf16),
            pltpu.VMEM((3 * list_size, list_size), bf16),
            pltpu.VMEM((2 * list_size, list_size), bf16),
            pltpu.VMEM((pixels, list_size), f32),
            pltpu.VMEM((pixels, list_size), f32),
            pltpu.VMEM((pixels, list_size), f32),
            pltpu.VMEM((group * 32, list_size), bf16),
            pltpu.VMEM((blocks // group, group * 32, 128), f32),
        ],
        compiler_params=pltpu.CompilerParams(vmem_limit_bytes=limit),
        name="composite_tiles",
    )(first_tile, lengths[0], lists[0], target[0], table)

    row_grads = pl.pallas_call(
        lambda *refs: collect_kernel(peers, tile_groups, *refs),
        out_shape=jax.ShapeDtypeStruct((view_count, 9, owned), f32),
        in_specs=in_vmem(1),
        out_specs=pl.BlockSpec(memory_space=pltpu.VMEM),
        scratch_shapes=[
            pltpu.VMEM((peers, 9, owned), f32),
            pltpu.SemaphoreType.DMA((peers,)),
            pltpu.SemaphoreType.DMA((peers,)),
        ],
        compiler_params=pltpu.CompilerParams(
            collective_id=1, has_side_effects=True, vmem_limit_bytes=limit
        ),
        name="collect_grads",
    )(dense)

    like = jax.ShapeDtypeStruct(params.shape, f32)
    return pl.pallas_call(
        lambda *refs: update_kernel(width, height, *refs),
        out_shape=(like, like, like),
        in_specs=in_vmem(6),
        out_specs=tuple(in_vmem(3)),
        compiler_params=pltpu.CompilerParams(vmem_limit_bytes=limit),
        name="update_gaussians",
    )(cameras, jnp.asarray(learning), row_grads, params, first_moment, second_moment)


def solution(mesh):
    placed = (
        P(None, ("views", "tiles")),
        P(None, ("views", "tiles")),
        P(None, ("views", "tiles")),
        P(),
        P("views", "tiles", None, None),
        P("views", "tiles", None),
        P("views", "tiles"),
    )
    return jax.shard_map(
        per_device,
        mesh=mesh,
        in_specs=placed,
        out_specs=(
            P(None, ("views", "tiles")),
            P(None, ("views", "tiles")),
            P(None, ("views", "tiles")),
        ),
        check_vma=False,
    )
```

time: 517 us -> 56.1 us (0.11)
  other arithmetic: 222 us -> 0 us
  waiting for transfers between devices: 131 us -> 0 us
  between operations: 55.8 us -> 0.65 us
  Pallas kernels: 0 us -> 53.6 us
  local copies, waits for them, and re-layouts: 54.7 us -> 1.45 us
  blocking collectives: 48.3 us -> 0 us
    reduce_scatter x1 -> x0, waiting for transfers between devices: 131 us -> none  [per_device(): lax.psum_scatter(spread_rows(row_grads, entries, owned // 128 * lax.axis_...]
    another operation x25 -> x0, other arithmetic: 64.2 us -> none
    pallas_call x0 -> x4, Pallas kernels: none -> 53.6 us  [the longest x1 27 us: per_device(): pl.pallas_call(composite_kernel, out_shape=jax.ShapeDtypeStruct((peers, 9...]
    all_gather x1 -> x0, blocking collectives: 48.3 us -> none  [per_device(): lax.all_gather(projected, ('views', 'tiles'), axis=2, tiled=True)]
    reduce_sum x14 -> x0, other arithmetic: 32.7 us -> none  [the longest x4 11.3 us: composite(): jnp.sum(weight * picked[6 + channel][:, :, None], axis=1)]
    mul x48 -> x0, other arithmetic: 28.5 us -> none  [the longest x16 12.4 us: project(): basis[coef_at] * params[11 + 3 * coef_at + channel]]
    scatter-add x1 -> x0, other arithmetic: 24 us -> none  [spread_rows(): dense_rows.at[:, jnp.clip(positions, 0, width_here - 1)]]
    select_n x10 -> x0, other arithmetic: 21.4 us -> none  [the longest x4 17.7 us: composite(): jnp.where(live_mask[:, :, None], picked[5][:, :, None] * jnp.exp(-0.5 * q...]
  transfers between devices with their start and end apart: 1 -> 0, of which waited for: 1 -> 0; matrix products, arithmetic and copies ran while one was open for 0% -> 0% of each run, Pallas kernels for 0% -> 0%
where the time goes in v1:
time: 56.1 us; the launch traced here: 55.7 us
  Pallas kernels  53.6 us (96%)
  local copies, waits for them, and re-layouts  1.45 us (3%)
  between operations  0.65 us (1%)
    pallas_call x1, Pallas kernels, per_device(): pl.pallas_call(composite_kernel, out_shape=jax.ShapeDtypeStruct((peers, 9...  27 us
    pallas_call x1, Pallas kernels, per_device(): pl.pallas_call(lambda *refs: project_kernel(peers, tile_groups, width, he...  13.6 us
    pallas_call x1, Pallas kernels, per_device(): pl.pallas_call(lambda *refs: collect_kernel(peers, tile_groups, *refs), o...  11.1 us
    pallas_call x1, Pallas kernels, per_device(): pl.pallas_call(lambda *refs: update_kernel(width, height, *refs), out_sha...  1.97 us
    unnamed x1, local copies, waits for them, and re-layouts  1.45 us

profile of v1, /device:TPU:0, one launch (start us, length us, event | category | flops | bytes accessed | tf_op | source)
XLA Modules:
  0.0 55.7 jit_solution(14023444204880436900)
XLA Ops:
  0.6 1.5 %copy.13 = f32[1,16,3,256]{3,2,1,0:T(4,128)} copy(f32[1,16,3,256]{3,1,2,0:T(8,128)} %param.12) | data formatting | bytes 98304 | tf_op args[4]
  2.1 13.6 %project_rows.1.table_ref = f32[32,9,128]{2,1,0:T(8,128)} custom-call(f32[4,6]{1,0:T(4,128)} %refs_0_.3, f32[59,128]{1,0:T(8,128)} %refs_3_.1), custom_call_target="tpu_custom_call" | custom-call | tf_op jit(solution)/shard_map/project_rows/pallas_call | solution.py:499
  15.7 27.0 %composite_tiles.1.refs_0_ = f32[32,9,128]{2,1,0:T(8,128)} custom-call(s32[1]{0:T(128)} %bitcast.first_tile_ref, s32[16]{0:T(128)} %bitcast.8, s32[16,256]{1,0:T(8,128)} %bitcast.7, f32[16,3,256]{2,1,0:T(4,128)} %bitcast.6, f32[32,9,128]{2,1,0:T(8,128)} %project_rows.1.table_ref), custom_call_target="tpu_custom_call" | custom-call | tf_op jit(solution)/shard_map/composite_tiles/pallas_call | solution.py:518
  42.7 11.1 %collect_grads.1.refs_2_ = f32[4,9,128]{2,1,0:T(8,128)} custom-call(f32[32,9,128]{2,1,0:T(8,128)} %composite_tiles.1.refs_0_), custom_call_target="tpu_custom_call" | custom-call | tf_op jit(solution)/shard_map/collect_grads/pallas_call | solution.py:539
  53.8 2.0 %update_gaussians.1 = (f32[59,128]{1,0:T(8,128)}, f32[59,128]{1,0:T(8,128)}, f32[59,128]{1,0:T(8,128)}) custom-call(f32[4,6]{1,0:T(4,128)} %refs_0_.3, f32[59,1]{1,0:T(8,128)} %constant.8.clone.refs_1_, f32[4,9,128]{2,1,0:T(8,128)} %collect_grads.1.refs_2_, f32[59,128]{1,0:T(8,128)} %refs_3_.1, f32[59,128]{1,0:T(8,128)} %refs_4_.1, f32[59,128]{1,0:T(8,128)} %refs_5_.1), custom_call_target="tpu_custom_call" | custom-call | tf_op jit(solution)/shard_map/update_gaussians/pallas_call | solution.py:556

commit v2 on v1

v2 whole, which is shorter than its diff:
```python
import jax
import jax.numpy as jnp
import numpy as np
from jax import lax
from jax.experimental import pallas as pl
from jax.experimental.pallas import tpu as pltpu
from jax.sharding import PartitionSpec as P

TILE_SIDE = 16
TILE_COLS = 32
ADAM_STEP = 1000


sh_zero = 0.28209479177387814
sh_first = 0.4886025119029199
sh_second = (
    1.0925484305920792,
    -1.0925484305920792,
    0.31539156525252005,
    -1.0925484305920792,
    0.5462742152960396,
)
sh_third = (
    -0.5900435899266435,
    2.890611442640554,
    -0.4570457994644658,
    0.3731763325901154,
    -0.4570457994644658,
    1.445305721320277,
    -0.5900435899266435,
)
beta_one = 0.9
beta_two = 0.999
adam_eps = 1e-15
learning = np.concatenate(
    [
        np.full(3, 0.00016),
        np.full(3, 0.005),
        np.full(4, 0.001),
        np.full(1, 0.05),
        np.full(3, 0.0025),
        np.full(45, 0.000125),
    ]
).astype(np.float32)[:, None]


def matmul_three(left, right):
    return [
        [
            left[row_at][0] * right[0][col_at]
            + left[row_at][1] * right[1][col_at]
            + left[row_at][2] * right[2][col_at]
            for col_at in range(3)
        ]
        for row_at in range(3)
    ]


def camera_rotation(camera):
    cos_a, sin_a = (jnp.cos(camera[0]), jnp.sin(camera[0]))
    cos_b, sin_b = (jnp.cos(camera[1]), jnp.sin(camera[1]))
    cos_c, sin_c = (jnp.cos(camera[2]), jnp.sin(camera[2]))
    around_x = [[1.0, 0.0, 0.0], [0.0, cos_a, -sin_a], [0.0, sin_a, cos_a]]
    around_y = [[cos_b, 0.0, sin_b], [0.0, 1.0, 0.0], [-sin_b, 0.0, cos_b]]
    around_z = [[cos_c, -sin_c, 0.0], [sin_c, cos_c, 0.0], [0.0, 0.0, 1.0]]
    return matmul_three(around_z, matmul_three(around_y, around_x))


def sh_basis(along_x, along_y, along_z):
    square_x, square_y, square_z = (along_x * along_x, along_y * along_y, along_z * along_z)
    both_xy, both_yz, both_xz = (along_x * along_y, along_y * along_z, along_x * along_z)
    return [
        sh_zero + 0.0 * along_x,
        -sh_first * along_y,
        sh_first * along_z,
        -sh_first * along_x,
        sh_second[0] * both_xy,
        sh_second[1] * both_yz,
        sh_second[2] * (2.0 * square_z - square_x - square_y),
        sh_second[3] * both_xz,
        sh_second[4] * (square_x - square_y),
        sh_third[0] * along_y * (3.0 * square_x - square_y),
        sh_third[1] * both_xy * along_z,
        sh_third[2] * along_y * (4.0 * square_z - square_x - square_y),
        sh_third[3] * along_z * (2.0 * square_z - 3.0 * square_x - 3.0 * square_y),
        sh_third[4] * along_x * (4.0 * square_z - square_x - square_y),
        sh_third[5] * along_z * (square_x - square_y),
        sh_third[6] * along_x * (square_x - 3.0 * square_y),
    ]


def project(rows, camera, focal_len, center_x, center_y):
    rotation = camera_rotation(camera)
    means = rows[0:3]
    point = [
        rotation[axis_at][0] * means[0]
        + rotation[axis_at][1] * means[1]
        + rotation[axis_at][2] * means[2]
        + camera[3 + axis_at]
        for axis_at in range(3)
    ]
    inverse_z = 1.0 / point[2]
    screen_u = focal_len * point[0] * inverse_z + center_x
    screen_v = focal_len * point[1] * inverse_z + center_y
    scales = [jnp.exp(value) for value in rows[3:6]]
    norm = rows[6] * rows[6] + rows[7] * rows[7] + rows[8] * rows[8] + rows[9] * rows[9]
    inverse_norm = lax.rsqrt(norm)
    real_part, imag_x, imag_y, imag_z = [value * inverse_norm for value in rows[6:10]]
    spin = [
        [
            1.0 - 2.0 * (imag_y * imag_y + imag_z * imag_z),
            2.0 * (imag_x * imag_y - real_part * imag_z),
            2.0 * (imag_x * imag_z + real_part * imag_y),
        ],
        [
            2.0 * (imag_x * imag_y + real_part * imag_z),
            1.0 - 2.0 * (imag_x * imag_x + imag_z * imag_z),
            2.0 * (imag_y * imag_z - real_part * imag_x),
        ],
        [
            2.0 * (imag_x * imag_z - real_part * imag_y),
            2.0 * (imag_y * imag_z + real_part * imag_x),
            1.0 - 2.0 * (imag_x * imag_x + imag_y * imag_y),
        ],
    ]
    turned = matmul_three(rotation, spin)
    shaped = [
        [turned[row_at][col_at] * scales[col_at] for col_at in range(3)] for row_at in range(3)
    ]
    near_x = [
        focal_len * inverse_z * shaped[0][col_at]
        - focal_len * point[0] * inverse_z * inverse_z * shaped[2][col_at]
        for col_at in range(3)
    ]
    near_y = [
        focal_len * inverse_z * shaped[1][col_at]
        - focal_len * point[1] * inverse_z * inverse_z * shaped[2][col_at]
        for col_at in range(3)
    ]
    cov_a = near_x[0] * near_x[0] + near_x[1] * near_x[1] + near_x[2] * near_x[2] + 0.3
    cov_b = near_x[0] * near_y[0] + near_x[1] * near_y[1] + near_x[2] * near_y[2]
    cov_c = near_y[0] * near_y[0] + near_y[1] * near_y[1] + near_y[2] * near_y[2] + 0.3
    determinant = cov_a * cov_c - cov_b * cov_b
    offset = [
        means[axis_at]
        + rotation[0][axis_at] * camera[3]
        + rotation[1][axis_at] * camera[4]
        + rotation[2][axis_at] * camera[5]
        for axis_at in range(3)
    ]
    inverse_len = lax.rsqrt(offset[0] * offset[0] + offset[1] * offset[1] + offset[2] * offset[2])
    basis = sh_basis(offset[0] * inverse_len, offset[1] * inverse_len, offset[2] * inverse_len)
    colors = [
        0.5 + sum((basis[coef_at] * rows[11 + 3 * coef_at + channel] for coef_at in range(16)))
        for channel in range(3)
    ]
    return (
        screen_u,
        screen_v,
        cov_c / determinant,
        -cov_b / determinant,
        cov_a / determinant,
        colors[0],
        colors[1],
        colors[2],
    )


def rotated(start, count):
    return [lax.rem(start + step, count) for step in range(count)]


def greet(views, tiles):
    barrier = pltpu.get_barrier_semaphore()
    here = (views[0], tiles[0])
    others = [(view, here[1]) for view in views[1:]] + [(here[0], tile) for tile in tiles[1:]]
    for device in others:
        pl.semaphore_signal(
            barrier, inc=1, device_id=device, device_id_type=pl.DeviceIdType.MESH
        )
    return lambda: pl.semaphore_wait(barrier, len(others))


def send(source, landing, send_sem, recv_sem, device):
    copy = pltpu.make_async_remote_copy(
        src_ref=source,
        dst_ref=landing,
        send_sem=send_sem,
        recv_sem=recv_sem,
        device_id=device,
        device_id_type=pl.DeviceIdType.MESH,
    )
    copy.start()
    return copy


def camera_columns(cameras_ref):
    return [cameras_ref[:, at : at + 1] for at in range(6)]


def sigmoid(value):
    return 1.0 / (1.0 + jnp.exp(-value))


def fold(value):
    return value[0:8] + value[8:16]


def wide(row):
    eight = jnp.broadcast_to(row, (8, row.shape[1]))
    return jnp.concatenate([eight, eight], axis=0)


def step_kernel(
    width,
    height,
    lengths_ref,
    cameras_ref,
    params_ref,
    lists_ref,
    target_ref,
    out_ref,
    rows_ref,
    table_ref,
    dense_ref,
    landing_ref,
    summed_ref,
    view_send,
    view_recv,
    tile_send,
    tile_recv,
    view_send_back,
    view_recv_back,
    tile_send_back,
    tile_recv_back,
    picked,
    keeps,
    suffix,
    before,
    after,
    alpha_s,
    ratio_s,
    flow_s,
    chosen,
    one_hot,
    spread,
):
    f32, bf16 = jnp.float32, jnp.bfloat16
    tile_dev, list_size = lists_ref.shape
    tile_groups, view_count, _, owned = table_ref.shape
    per_owner = owned // 128
    halves = list_size // 128
    views = rotated(lax.axis_index("views"), view_count)
    tiles = rotated(lax.axis_index("tiles"), tile_groups)
    everyone_here = greet(views, tiles)
    values = [params_ref[at : at + 1, :] for at in range(59)]
    made = project(
        values, camera_columns(cameras_ref), float(width), 0.5 * width, 0.5 * height
    )
    opacities = jnp.broadcast_to(sigmoid(values[10]), (view_count, owned))
    for row_at, value in enumerate(made[:5] + (opacities,) + made[5:]):
        rows_ref[:, row_at, :] = value
    everyone_here()
    mine = table_ref.at[tiles[0]]
    over_views = [
        send(
            rows_ref.at[view],
            mine.at[views[0]],
            view_send.at[at],
            view_recv.at[at],
            (view, tiles[0]),
        )
        for at, view in enumerate(views[1:])
    ]
    table_ref[pl.ds(tiles[0], 1), pl.ds(views[0], 1)] = rows_ref[pl.ds(views[0], 1)][None]
    for copy in over_views:
        copy.wait()
    over_tiles = [
        send(mine, mine, tile_send.at[at], tile_recv.at[at], (views[0], tile))
        for at, tile in enumerate(tiles[1:])
    ]

    row_ids = lax.broadcasted_iota(jnp.int32, (list_size, list_size), 0)
    col_ids = lax.broadcasted_iota(jnp.int32, (list_size, list_size), 1)
    for piece in range(2):
        here = slice(piece * list_size, (piece + 1) * list_size)
        before[here, :] = (row_ids < col_ids).astype(f32).astype(bf16)
        after[here, :] = (row_ids > col_ids).astype(f32).astype(bf16)
    spread[...] = jnp.zeros_like(spread)
    lane_ids = lax.broadcasted_iota(jnp.int32, (1, list_size), 1)
    pixel_ids = lax.broadcasted_iota(jnp.int32, (16, list_size), 0).astype(f32)
    column_ids = lax.broadcasted_iota(jnp.int32, (256, list_size), 0)
    first_tile = tiles[0] * tile_dev
    entries = lists_ref[...]
    block_of = entries >> 7
    column_of = entries & 127

    def gather_from(tile_group, carry):
        carry = list(carry)
        for view in range(view_count):
            for part in range(per_owner):
                lanes = slice(part * 128, part * 128 + 128)
                block = (view * tile_groups + tile_group) * per_owner + part
                for half in range(halves):
                    here = slice(half * 128, half * 128 + 128)
                    mask = block_of[:, here] == block
                    column = column_of[:, here]
                    for row_at in range(9):
                        line = table_ref[tile_group, view, row_at : row_at + 1, lanes]
                        got = jnp.take_along_axis(
                            jnp.broadcast_to(line, (tile_dev, 128)),
                            column,
                            axis=1,
                            mode="promise_in_bounds",
                        )
                        slot = half * 9 + row_at
                        carry[slot] = jnp.where(mask, got, carry[slot])
        return tuple(carry)

    def gather_arrived(at, carry):
        source = lax.rem(tiles[0] + tile_groups - at, tile_groups)
        pltpu.make_async_remote_copy(
            src_ref=mine,
            dst_ref=table_ref.at[source],
            send_sem=tile_send.at[at - 1],
            recv_sem=tile_recv.at[at - 1],
            device_id=(views[0], source),
            device_id_type=pl.DeviceIdType.MESH,
        ).wait_recv()
        return gather_from(source, carry)

    gathered = tuple(jnp.zeros((tile_dev, 128), f32) for _ in range(halves * 9))
    gathered = gather_from(tiles[0], gathered)
    gathered = lax.fori_loop(1, tile_groups, gather_arrived, gathered)
    for half in range(halves):
        for row_at in range(9):
            picked[row_at, :, half * 128 : half * 128 + 128] = gathered[half * 9 + row_at]
    for copy in over_tiles:
        copy.wait_send()
    group = spread.shape[1] // 32
    pair = keeps.shape[0]
    lines = [slice(line * 16, line * 16 + 16) for line in range(TILE_SIDE)]

    def load_tile(tile_at):
        tile_id = first_tile + tile_at
        left = (tile_id % TILE_COLS * TILE_SIDE).astype(f32) + 0.5
        top = (tile_id // TILE_COLS * TILE_SIDE).astype(f32) + 0.5
        rows = [picked[row_at, pl.ds(tile_at, 1), :] for row_at in range(9)]
        rows[5] = jnp.where(lane_ids < lengths_ref[tile_at], rows[5], 0.0)
        delta_x = (pixel_ids + left) - wide(rows[0])
        return rows, delta_x, top

    def delta_y_at(rows, top, line):
        return (top + float(line)) - wide(rows[1])

    def alphas_of(slot, rows, delta_x, top):
        opacity = wide(rows[5])
        part_a = wide(-0.5 * rows[2]) * delta_x * delta_x
        part_b = wide(-rows[3]) * delta_x
        half_c = wide(-0.5 * rows[4])
        for line, here in enumerate(lines):
            delta_y = delta_y_at(rows, top, line)
            alphas = opacity * jnp.exp(part_a + delta_y * (part_b + half_c * delta_y))
            log_keep = jnp.log(1.0 - alphas)
            high = log_keep.astype(bf16)
            keeps[slot, here, 0:list_size] = high
            keeps[slot, here, list_size : 2 * list_size] = (log_keep - high.astype(f32)).astype(bf16)
            alpha_s[slot, here, :] = alphas
            ratio_s[slot, here, :] = alphas * jnp.exp(-log_keep)

    def weights_of(slot, tile_at, rows, passed):
        wanted = jnp.concatenate(
            [target_ref[channel, pl.ds(tile_at, 1), :] for channel in range(3)]
            + [jnp.zeros((5, TILE_SIDE * TILE_SIDE), f32)],
            axis=0,
        ).T
        colors = [wide(row) for row in rows[6:9]]
        color_sums = [jnp.zeros((8, list_size), f32) for _ in range(3)]
        for here in lines:
            weight = jnp.exp(passed[here]) * alpha_s[slot, here, :]
            flow = None
            for channel, color in enumerate(colors):
                colored = weight * color
                gap = jnp.sum(colored, axis=1, keepdims=True) - wanted[here, channel : channel + 1]
                sign = jnp.where(gap > 0.0, 1.0, jnp.where(gap < 0.0, -1.0, 0.0))
                sign = jnp.broadcast_to(sign, colored.shape)
                color_sums[channel] = color_sums[channel] + fold(weight * sign)
                flow = colored * sign if flow is None else flow + colored * sign
            high = flow.astype(bf16)
            suffix[slot, here, 0:list_size] = high
            suffix[slot, here, list_size : 2 * list_size] = (flow - high.astype(f32)).astype(bf16)
            flow_s[slot, here, :] = flow
        return color_sums

    def grads_of(slot, rows, delta_x, top, behind, color_sums):
        sums = [jnp.zeros((8, list_size), f32) for _ in range(6)]
        for line, here in enumerate(lines):
            delta_y = delta_y_at(rows, top, line)[0:8]
            pull = flow_s[slot, here, :] - behind[here] * ratio_s[slot, here, :]
            pull_x = pull * delta_x
            pull_xx = fold(pull_x * delta_x)
            pull_x = fold(pull_x)
            pull = fold(pull)
            pull_y = pull * delta_y
            terms = (pull, pull_x, pull_y, pull_xx, pull_x * delta_y, pull_y * delta_y)
            sums = [total + term for total, term in zip(sums, terms)]
        flat, by_x, by_y, by_xx, by_xy, by_yy = [
            jnp.sum(total, axis=0, keepdims=True) for total in sums
        ]
        _, _, con_a, con_b, con_c = rows[:5]
        return jnp.concatenate(
            [
                con_a * by_x + con_b * by_y,
                con_b * by_x + con_c * by_y,
                -0.5 * by_xx,
                -by_xy,
                -0.5 * by_yy,
                flat,
            ]
            + [jnp.sum(total, axis=0, keepdims=True) for total in color_sums]
            + [jnp.zeros((7, list_size), f32)],
            axis=0,
        )

    def some_tiles(step, carry):
        slots = range(pair)
        at = [step * pair + slot for slot in slots]
        tiles = [load_tile(tile_at) for tile_at in at]
        for slot in slots:
            alphas_of(slot, *tiles[slot])
        passed = [jnp.dot(keeps[slot], before[...], preferred_element_type=f32) for slot in slots]
        color_sums = [weights_of(slot, at[slot], tiles[slot][0], passed[slot]) for slot in slots]
        behind = [jnp.dot(suffix[slot], after[...], preferred_element_type=f32) for slot in slots]
        owners, pieces = [], []
        for slot in slots:
            grads = grads_of(slot, *tiles[slot], behind[slot], color_sums[slot])
            high = grads.astype(bf16).astype(f32)
            pieces.append(jnp.concatenate([high, grads - high], axis=0))
            ids = lists_ref[pl.ds(at[slot], 1), :]
            owners.append(wide(ids >> 8))
            lanes = slice(slot * list_size, (slot + 1) * list_size)
            one_hot[:, lanes] = (column_ids == (ids & 255)).astype(f32).astype(bf16)

        def spread_group(group_at, carry):
            for slot in slots:
                lanes = slice(slot * list_size, (slot + 1) * list_size)
                for block in range(group):
                    mask = owners[slot] == group_at * group + block
                    mask = jnp.concatenate([mask, mask], axis=0)
                    chosen[block * 32 : block * 32 + 32, lanes] = jnp.where(
                        mask, pieces[slot], 0.0
                    ).astype(bf16)
            spread[group_at] += lax.dot_general(
                chosen[...], one_hot[...], (((1,), (1,)), ((), ())), preferred_element_type=f32
            )
            return carry

        if spread.shape[0] == 1:
            spread_group(0, 0)
        else:
            lax.fori_loop(0, spread.shape[0], spread_group, 0)
        return carry

    lax.fori_loop(0, tile_dev // pair, some_tiles, 0)

    def finish_group(group_at, carry):
        for block in range(group):
            both = spread[group_at, block * 32 : block * 32 + 32, :]
            total = both[0:16] + both[16:32]
            for half in range(2):
                chunk = block * 2 + half
                owner = group_at * (2 * group // per_owner) + chunk // per_owner
                lanes = chunk % per_owner * 128
                dense_ref[owner % tile_groups, owner // tile_groups, :, lanes : lanes + 128] = total[
                    0:9, half * 128 : half * 128 + 128
                ]
        return carry

    if spread.shape[0] == 1:
        finish_group(0, 0)
    else:
        lax.fori_loop(0, spread.shape[0], finish_group, 0)

    over_tiles = [
        send(
            dense_ref.at[tile],
            landing_ref.at[at],
            tile_send_back.at[at],
            tile_recv_back.at[at],
            (views[0], tile),
        )
        for at, tile in enumerate(tiles[1:])
    ]
    total = dense_ref[pl.ds(tiles[0], 1)][0]
    for at, copy in enumerate(over_tiles):
        copy.wait()
        total = total + landing_ref[at]
    summed_ref[...] = total
    over_views = [
        send(
            summed_ref.at[view],
            out_ref.at[views[0]],
            view_send_back.at[at],
            view_recv_back.at[at],
            (view, tiles[0]),
        )
        for at, view in enumerate(views[1:])
    ]
    out_ref[pl.ds(views[0], 1)] = summed_ref[pl.ds(views[0], 1)]
    for copy in over_views:
        copy.wait()


def update_kernel(
    width,
    height,
    cameras_ref,
    rates_ref,
    grads_ref,
    params_ref,
    first_ref,
    second_ref,
    new_params_ref,
    new_first_ref,
    new_second_ref,
):
    camera = camera_columns(cameras_ref)
    values = [params_ref[at : at + 1, :] for at in range(59)]
    _, pullback = jax.vjp(
        lambda rows: project(rows, camera, float(width), 0.5 * width, 0.5 * height), values
    )
    given = [grads_ref[:, row_at, :] for row_at in range(9)]
    grads = list(pullback(tuple(given[:5] + given[6:]))[0])
    grads[10] = jnp.sum(given[5], axis=0, keepdims=True) * (1.0 - sigmoid(values[10]))
    for at in range(59):
        new_first_ref[at : at + 1, :] = grads[at]
    gradient = new_first_ref[...]
    new_first = beta_one * first_ref[...] + (1.0 - beta_one) * gradient
    new_second = beta_two * second_ref[...] + (1.0 - beta_two) * gradient * gradient
    new_first_ref[...] = new_first
    new_second_ref[...] = new_second
    step_size = rates_ref[...] * (new_first / (1.0 - beta_one**ADAM_STEP))
    new_params_ref[...] = params_ref[...] - step_size / (
        jnp.sqrt(new_second / (1.0 - beta_two**ADAM_STEP)) + adam_eps
    )


def in_vmem(count):
    return [pl.BlockSpec(memory_space=pltpu.VMEM)] * count


def per_device(params, first_moment, second_moment, cameras, target, lists, lengths):
    f32, bf16 = jnp.float32, jnp.bfloat16
    view_count = lax.axis_size("views")
    tile_groups = lax.axis_size("tiles")
    peers = view_count * tile_groups
    owned = params.shape[1]
    tile_dev = target.shape[1]
    list_size = lists.shape[2]
    pixels = target.shape[3]
    width = TILE_COLS * TILE_SIDE
    height = tile_dev * tile_groups // TILE_COLS * TILE_SIDE
    limit = 40 * 1024 * 1024

    dma = pltpu.SemaphoreType.DMA
    semaphores = [
        dma((view_count,)),
        dma((view_count,)),
        dma((tile_groups,)),
        dma((tile_groups,)),
    ]
    by_owner = (tile_groups, view_count, 9, owned)
    block_rows = (view_count, 9, owned)
    blocks = peers * owned // 256
    group = 16
    pair = 2
    row_grads = pl.pallas_call(
        lambda *refs: step_kernel(width, height, *refs),
        out_shape=jax.ShapeDtypeStruct(block_rows, f32),
        in_specs=[pl.BlockSpec(memory_space=pltpu.SMEM)] + in_vmem(4),
        out_specs=pl.BlockSpec(memory_space=pltpu.VMEM),
        scratch_shapes=[
            pltpu.VMEM(block_rows, f32),
            pltpu.VMEM(by_owner, f32),
            pltpu.VMEM(by_owner, f32),
            pltpu.VMEM((tile_groups - 1,) + block_rows, f32),
            pltpu.VMEM(block_rows, f32),
        ]
        + semaphores
        + semaphores
        + [
            pltpu.VMEM((9, tile_dev, list_size), f32),
            pltpu.VMEM((pair, pixels, 2 * list_size), bf16),
            pltpu.VMEM((pair, pixels, 2 * list_size), bf16),
            pltpu.VMEM((2 * list_size, list_size), bf16),
            pltpu.VMEM((2 * list_size, list_size), bf16),
            pltpu.VMEM((pair, pixels, list_size), f32),
            pltpu.VMEM((pair, pixels, list_size), f32),
            pltpu.VMEM((pair, pixels, list_size), f32),
            pltpu.VMEM((group * 32, pair * list_size), bf16),
            pltpu.VMEM((256, pair * list_size), bf16),
            pltpu.VMEM((blocks // group, group * 32, 256), f32),
        ],
        compiler_params=pltpu.CompilerParams(
            collective_id=0, has_side_effects=True, vmem_limit_bytes=limit
        ),
        name="splat_gradients",
    )(lengths[0], cameras, params, lists[0], target[0].transpose(1, 0, 2))

    like = jax.ShapeDtypeStruct(params.shape, f32)
    return pl.pallas_call(
        lambda *refs: update_kernel(width, height, *refs),
        out_shape=(like, like, like),
        in_specs=in_vmem(6),
        out_specs=tuple(in_vmem(3)),
        compiler_params=pltpu.CompilerParams(vmem_limit_bytes=limit // 4),
        name="update_gaussians",
    )(cameras, jnp.asarray(learning), row_grads, params, first_moment, second_moment)


def solution(mesh):
    placed = (
        P(None, ("views", "tiles")),
        P(None, ("views", "tiles")),
        P(None, ("views", "tiles")),
        P(),
        P("views", "tiles", None, None),
        P("views", "tiles", None),
        P("views", "tiles"),
    )
    return jax.shard_map(
        per_device,
        mesh=mesh,
        in_specs=placed,
        out_specs=(
            P(None, ("views", "tiles")),
            P(None, ("views", "tiles")),
            P(None, ("views", "tiles")),
        ),
        check_vma=False,
    )
```

time: 56.1 us -> 42.1 us (0.75)
  Pallas kernels: 53.6 us -> 38.2 us
  local copies, waits for them, and re-layouts: 1.45 us -> 2.95 us
    pallas_call x3 -> x1, Pallas kernels: 51.7 us -> 37.1 us  [per_device(): pl.pallas_call(lambda *refs: step_kernel(width, height, *refs), out_shape...]
    unnamed x1 -> x16, local copies, waits for them, and re-layouts: 1.45 us -> 2.95 us
    pallas_call x1, Pallas kernels: 1.97 us -> 1.12 us  [per_device(): pl.pallas_call(lambda *refs: update_kernel(width, height, *refs), out_sha...]
where the time goes in v2:
time: 42.1 us; the launch traced here: 41.8 us
  Pallas kernels  38.2 us (91%)
  local copies, waits for them, and re-layouts  2.95 us (7%)
  between operations  0.69 us (2%)
    pallas_call x1, Pallas kernels, per_device(): pl.pallas_call(lambda *refs: step_kernel(width, height, *refs), out_shape...  37.1 us
    unnamed x16, local copies, waits for them, and re-layouts  2.95 us
    pallas_call x1, Pallas kernels, per_device(): pl.pallas_call(lambda *refs: update_kernel(width, height, *refs), out_sha...  1.12 us

profile of v2, /device:TPU:0, one launch (start us, length us, event | category | flops | bytes accessed | tf_op | source)
XLA Modules:
  0.0 41.8 jit_solution(9588413192249457724)
XLA Ops:
  0.6 0.0 copy-start.6
  0.6 0.0 copy-start.7
  0.7 0.7 %copy-done.6 = f32[4,6]{1,0:T(4,128)S(1)} copy-done((f32[4,6]{1,0:T(4,128)S(1)}, f32[4,6]{1,0:T(4,128)}, u32[]{:S(2)}) %copy-start.6) | copy-done | bytes 120
  1.3 0.0 copy-done.7
  1.3 0.0 copy-start
  1.3 0.8 %copy-done = f32[59,128]{1,0:T(8,128)S(1)} copy-done((f32[59,128]{1,0:T(8,128)S(1)}, f32[59,128]{1,0:T(8,128)}, u32[]{:S(2)}) %copy-start) | copy-done | bytes 30232
  2.1 0.0 copy-start.1
  2.1 0.8 %copy-done.1 = f32[1,16,3,256]{3,1,2,0:T(8,128)S(1)} copy-done((f32[1,16,3,256]{3,1,2,0:T(8,128)S(1)}, f32[1,16,3,256]{3,1,2,0:T(8,128)}, u32[]{:S(2)}) %copy-start.1) | copy-done | bytes 49176
  2.9 0.0 copy-start.5
  2.9 0.7 %copy-done.5 = s32[1,16,256]{2,1,0:T(8,128)S(1)} copy-done((s32[1,16,256]{2,1,0:T(8,128)S(1)}, s32[1,16,256]{2,1,0:T(8,128)}, u32[]{:S(2)}) %copy-start.5) | copy-done | bytes 16408
  3.6 0.0 copy-start.2
  3.6 0.0 copy-start.3
  3.6 0.0 copy-start.4
  3.6 37.1 %splat_gradients.1.refs_2_ = f32[4,9,128]{2,1,0:T(8,128)S(1)} custom-call(s32[16]{0:T(128)S(1)} %bitcast.7, f32[4,6]{1,0:T(4,128)S(1)} %copy-done.6, f32[59,128]{1,0:T(8,128)S(1)} %copy-done, s32[16,256]{1,0:T(8,128)S(1)} %bitcast.6, f32[3,16,256]{2,1,0:T(8,128)S(1)} %bitcast.5), custom_call_target="tpu_custom_call" | custom-call | tf_op jit(solution)/shard_map/splat_gradients/pallas_call | solution.py:577
  40.7 0.0 copy-done.2
  40.7 0.0 copy-done.3
  40.7 0.0 copy-done.4
  40.7 1.1 %update_gaussians.1 = (f32[59,128]{1,0:T(8,128)}, f32[59,128]{1,0:T(8,128)}, f32[59,128]{1,0:T(8,128)}) custom-call(f32[4,6]{1,0:T(4,128)S(1)} %copy-done.6, f32[59,1]{1,0:T(8,128)S(1)} %copy-done.4, f32[4,9,128]{2,1,0:T(8,128)S(1)} %splat_gradients.1.refs_2_, f32[59,128]{1,0:T(8,128)S(1)} %copy-done, f32[59,128]{1,0:T(8,128)S(1)} %copy-done.2, ...), custom_call_target="tpu_custom_call" | custom-call | tf_op jit(solution)/shard_map/update_gaussians/pallas_call | solution.py:611
Async XLA Ops:
  0.6 0.7 %copy-start.6 = (f32[4,6]{1,0:T(4,128)S(1)}, f32[4,6]{1,0:T(4,128)}, u32[]{:S(2)}) copy-start(f32[4,6]{1,0:T(4,128)} %refs_0_.1) | copy-start | bytes 292
  0.6 0.7 %copy-start.7 = (s32[1,16]{1,0:T(1,128)S(1)}, s32[1,16]{1,0:T(1,128)}, u32[]{:S(2)}) copy-start(s32[1,16]{1,0:T(1,128)} %param.14) | copy-start | bytes 196
  1.3 0.8 %copy-start = (f32[59,128]{1,0:T(8,128)S(1)}, f32[59,128]{1,0:T(8,128)}, u32[]{:S(2)}) copy-start(f32[59,128]{1,0:T(8,128)} %refs_3_.1) | copy-start | bytes 90628
  2.1 0.8 %copy-start.1 = (f32[1,16,3,256]{3,1,2,0:T(8,128)S(1)}, f32[1,16,3,256]{3,1,2,0:T(8,128)}, u32[]{:S(2)}) copy-start(f32[1,16,3,256]{3,1,2,0:T(8,128)} %param.12) | copy-start | bytes 147460
  2.9 0.7 %copy-start.5 = (s32[1,16,256]{2,1,0:T(8,128)S(1)}, s32[1,16,256]{2,1,0:T(8,128)}, u32[]{:S(2)}) copy-start(s32[1,16,256]{2,1,0:T(8,128)} %param.13) | copy-start | bytes 49156
  3.6 37.1 %copy-start.2 = (f32[59,128]{1,0:T(8,128)S(1)}, f32[59,128]{1,0:T(8,128)}, u32[]{:S(2)}) copy-start(f32[59,128]{1,0:T(8,128)} %refs_4_.1) | copy-start | bytes 90628
  3.6 37.1 %copy-start.3 = (f32[59,128]{1,0:T(8,128)S(1)}, f32[59,128]{1,0:T(8,128)}, u32[]{:S(2)}) copy-start(f32[59,128]{1,0:T(8,128)} %refs_5_.1) | copy-start | bytes 90628
  3.6 37.1 %copy-start.4 = (f32[59,1]{1,0:T(8,128)S(1)}, f32[59,1]{1,0:T(8,128)}, u32[]{:S(2)}) copy-start(f32[59,1]{1,0:T(8,128)} %constant.2.clone.refs_1_) | copy-start | bytes 712

commit v3 on v2

--- a/solution.py
+++ b/solution.py
@@ -215,11 +215,16 @@
     width,
     height,
     lengths_ref,
+    cameras_far,
+    params_far,
+    lists_far,
+    target_far,
+    out_ref,
     cameras_ref,
     params_ref,
     lists_ref,
     target_ref,
-    out_ref,
+    fetch_sem,
     rows_ref,
     table_ref,
     dense_ref,
@@ -241,6 +246,10 @@
     alpha_s,
     ratio_s,
     flow_s,
+    weight_s,
+    painted,
+    paints,
+    tints,
     chosen,
     one_hot,
     spread,
@@ -252,7 +261,16 @@
     halves = list_size // 128
     views = rotated(lax.axis_index("views"), view_count)
     tiles = rotated(lax.axis_index("tiles"), tile_groups)
+    pairs = ((params_far, params_ref), (cameras_far, cameras_ref))
+    pairs = pairs + ((lists_far, lists_ref), (target_far, target_ref))
+    fetches = [
+        pltpu.make_async_copy(far, near, fetch_sem.at[at]) for at, (far, near) in enumerate(pairs)
+    ]
+    for fetch in fetches:
+        fetch.start()
     everyone_here = greet(views, tiles)
+    for fetch in fetches[:2]:
+        fetch.wait()
     values = [params_ref[at : at + 1, :] for at in range(59)]
     made = project(
         values, camera_columns(cameras_ref), float(width), 0.5 * width, 0.5 * height
@@ -287,10 +305,22 @@
         before[here, :] = (row_ids < col_ids).astype(f32).astype(bf16)
         after[here, :] = (row_ids > col_ids).astype(f32).astype(bf16)
     spread[...] = jnp.zeros_like(spread)
+    tints[...] = jnp.zeros_like(tints)
+    paints[...] = jnp.zeros_like(paints)
+    painted[:, :, 3 * list_size :] = jnp.zeros(
+        (painted.shape[0], painted.shape[1], 128), bf16
+    )
+    channels = lax.broadcasted_iota(jnp.int32, (16, 128), 0)
+    pieces_at = lax.broadcasted_iota(jnp.int32, (16, 128), 1)
+    same = (channels % 3 == pieces_at % 3) & (channels < 9) & (pieces_at < 9)
+    for slot in range(paints.shape[0]):
+        paints[slot, 0:16, 3 * list_size :] = jnp.where(same, -1.0, 0.0).astype(bf16)
     lane_ids = lax.broadcasted_iota(jnp.int32, (1, list_size), 1)
     pixel_ids = lax.broadcasted_iota(jnp.int32, (16, list_size), 0).astype(f32)
     column_ids = lax.broadcasted_iota(jnp.int32, (256, list_size), 0)
     first_tile = tiles[0] * tile_dev
+    for fetch in fetches[2:]:
+        fetch.wait()
     entries = lists_ref[...]
     block_of = entries >> 7
     column_of = entries & 127
@@ -368,29 +398,55 @@
             alpha_s[slot, here, :] = alphas
             ratio_s[slot, here, :] = alphas * jnp.exp(-log_keep)
 
-    def weights_of(slot, tile_at, rows, passed):
+    def split(value):
+        high = value.astype(bf16)
+        return high, (value - high.astype(f32)).astype(bf16)
+
+    def colors_of(slot, tile_at, rows):
+        empty = jnp.zeros((7, list_size), f32)
+        colors = jnp.concatenate(rows[6:9], axis=0)
+        high = colors.astype(bf16).astype(f32)
+        middle = (colors - high).astype(bf16).astype(f32)
+        low = colors - high - middle
+        highs = jnp.concatenate([high, high, high, empty], axis=0).astype(bf16)
+        lows = jnp.concatenate([middle, middle, middle, empty], axis=0).astype(bf16)
+        paints[slot, 0:16, 0:list_size] = highs
+        paints[slot, 0:16, list_size : 2 * list_size] = highs
+        paints[slot, 0:16, 2 * list_size : 3 * list_size] = lows
+        tints[slot, 0:16, :] = jnp.concatenate([high, middle, low, empty], axis=0).astype(bf16)
         wanted = jnp.concatenate(
-            [target_ref[channel, pl.ds(tile_at, 1), :] for channel in range(3)]
-            + [jnp.zeros((5, TILE_SIDE * TILE_SIDE), f32)],
-            axis=0,
-        ).T
-        colors = [wide(row) for row in rows[6:9]]
-        color_sums = [jnp.zeros((8, list_size), f32) for _ in range(3)]
+            [target_ref[channel, pl.ds(tile_at, 1), :] for channel in range(3)], axis=0
+        )
+        high = wanted.astype(bf16).astype(f32)
+        middle = (wanted - high).astype(bf16).astype(f32)
+        low = wanted - high - middle
+        wanted = jnp.concatenate([high, middle, low, jnp.zeros((7, wanted.shape[1]), f32)], axis=0)
+        painted[slot, :, 3 * list_size : 3 * list_size + 16] = wanted.T.astype(bf16)
+
+    def weights_of(slot, passed):
         for here in lines:
             weight = jnp.exp(passed[here]) * alpha_s[slot, here, :]
-            flow = None
-            for channel, color in enumerate(colors):
-                colored = weight * color
-                gap = jnp.sum(colored, axis=1, keepdims=True) - wanted[here, channel : channel + 1]
-                sign = jnp.where(gap > 0.0, 1.0, jnp.where(gap < 0.0, -1.0, 0.0))
-                sign = jnp.broadcast_to(sign, colored.shape)
-                color_sums[channel] = color_sums[channel] + fold(weight * sign)
-                flow = colored * sign if flow is None else flow + colored * sign
-            high = flow.astype(bf16)
+            high, low = split(weight)
+            weight_s[slot, here, :] = weight
+            painted[slot, here, 0:list_size] = high
+            painted[slot, here, list_size : 2 * list_size] = low
+            painted[slot, here, 2 * list_size : 3 * list_size] = high
+
+    def signs_of(gaps):
+        return jnp.where(gaps > 0.0, 1.0, jnp.where(gaps < 0.0, -1.0, 0.0))
+
+    def color_grads(slot, signs):
+        turned = signs.T[0:16].astype(bf16)
+        both = jnp.dot(turned, painted[slot, :, 0 : 2 * list_size], preferred_element_type=f32)
+        return both[0:3, 0:list_size] + both[0:3, list_size : 2 * list_size]
+
+    def flows_of(slot, tinted):
+        for here in lines:
+            flow = weight_s[slot, here, :] * tinted[here]
+            high, low = split(flow)
             suffix[slot, here, 0:list_size] = high
-            suffix[slot, here, list_size : 2 * list_size] = (flow - high.astype(f32)).astype(bf16)
+            suffix[slot, here, list_size : 2 * list_size] = low
             flow_s[slot, here, :] = flow
-        return color_sums
 
     def grads_of(slot, rows, delta_x, top, behind, color_sums):
         sums = [jnp.zeros((8, list_size), f32) for _ in range(6)]
@@ -417,7 +473,7 @@
                 -0.5 * by_yy,
                 flat,
             ]
-            + [jnp.sum(total, axis=0, keepdims=True) for total in color_sums]
+            + [color_sums]
             + [jnp.zeros((7, list_size), f32)],
             axis=0,
         )
@@ -425,15 +481,29 @@
     def some_tiles(step, carry):
         slots = range(pair)
         at = [step * pair + slot for slot in slots]
-        tiles = [load_tile(tile_at) for tile_at in at]
+        arrived = [load_tile(tile_at) for tile_at in at]
+        passed, gaps, tinted, color_sums, behind = [], [], [], [], []
         for slot in slots:
-            alphas_of(slot, *tiles[slot])
-        passed = [jnp.dot(keeps[slot], before[...], preferred_element_type=f32) for slot in slots]
-        color_sums = [weights_of(slot, at[slot], tiles[slot][0], passed[slot]) for slot in slots]
-        behind = [jnp.dot(suffix[slot], after[...], preferred_element_type=f32) for slot in slots]
+            alphas_of(slot, *arrived[slot])
+            passed.append(jnp.dot(keeps[slot], before[...], preferred_element_type=f32))
+            colors_of(slot, at[slot], arrived[slot][0])
+        for slot in slots:
+            weights_of(slot, passed[slot])
+            gaps.append(
+                lax.dot_general(
+                    painted[slot], paints[slot], (((1,), (1,)), ((), ())), preferred_element_type=f32
+                )
+            )
+        for slot in slots:
+            signs = signs_of(gaps[slot])
+            tinted.append(jnp.dot(signs.astype(bf16), tints[slot], preferred_element_type=f32))
+            color_sums.append(color_grads(slot, signs))
+        for slot in slots:
+            flows_of(slot, tinted[slot])
+            behind.append(jnp.dot(suffix[slot], after[...], preferred_element_type=f32))
         owners, pieces = [], []
         for slot in slots:
-            grads = grads_of(slot, *tiles[slot], behind[slot], color_sums[slot])
+            grads = grads_of(slot, *arrived[slot], behind[slot], color_sums[slot])
             high = grads.astype(bf16).astype(f32)
             pieces.append(jnp.concatenate([high, grads - high], axis=0))
             ids = lists_ref[pl.ds(at[slot], 1), :]
@@ -560,7 +630,7 @@
     pixels = target.shape[3]
     width = TILE_COLS * TILE_SIDE
     height = tile_dev * tile_groups // TILE_COLS * TILE_SIDE
-    limit = 40 * 1024 * 1024
+    limit = 56 * 1024 * 1024
 
     dma = pltpu.SemaphoreType.DMA
     semaphores = [
@@ -577,9 +647,15 @@
     row_grads = pl.pallas_call(
         lambda *refs: step_kernel(width, height, *refs),
         out_shape=jax.ShapeDtypeStruct(block_rows, f32),
-        in_specs=[pl.BlockSpec(memory_space=pltpu.SMEM)] + in_vmem(4),
+        in_specs=[pl.BlockSpec(memory_space=pltpu.SMEM)]
+        + [pl.BlockSpec(memory_space=pltpu.HBM)] * 4,
         out_specs=pl.BlockSpec(memory_space=pltpu.VMEM),
         scratch_shapes=[
+            pltpu.VMEM(cameras.shape, f32),
+            pltpu.VMEM(params.shape, f32),
+            pltpu.VMEM(lists.shape[1:], jnp.int32),
+            pltpu.VMEM((3, tile_dev, pixels), f32),
+            dma((4,)),
             pltpu.VMEM(block_rows, f32),
             pltpu.VMEM(by_owner, f32),
             pltpu.VMEM(by_owner, f32),
@@ -597,6 +673,10 @@
             pltpu.VMEM((pair, pixels, list_size), f32),
             pltpu.VMEM((pair, pixels, list_size), f32),
             pltpu.VMEM((pair, pixels, list_size), f32),
+            pltpu.VMEM((pair, pixels, list_size), f32),
+            pltpu.VMEM((pair, pixels, 3 * list_size + 128), bf16),
+            pltpu.VMEM((pair, 128, 3 * list_size + 128), bf16),
+            pltpu.VMEM((pair, 128, list_size), bf16),
             pltpu.VMEM((group * 32, pair * list_size), bf16),
             pltpu.VMEM((256, pair * list_size), bf16),
             pltpu.VMEM((blocks // group, group * 32, 256), f32),
@@ -613,7 +693,7 @@
         out_shape=(like, like, like),
         in_specs=in_vmem(6),
         out_specs=tuple(in_vmem(3)),
-        compiler_params=pltpu.CompilerParams(vmem_limit_bytes=limit // 4),
+        compiler_params=pltpu.CompilerParams(vmem_limit_bytes=limit),
         name="update_gaussians",
     )(cameras, jnp.asarray(learning), row_grads, params, first_moment, second_moment)
 

time: 42.1 us -> 39.5 us (0.938)
  local copies, waits for them, and re-layouts: 2.95 us -> 0 us
  Pallas kernels: 38.2 us -> 38.7 us
    unnamed x16 -> x0, local copies, waits for them, and re-layouts: 2.95 us -> none
    pallas_call x1, Pallas kernels: 1.12 us -> 1.97 us  [per_device(): pl.pallas_call(lambda *refs: update_kernel(width, height, *refs), out_sha...]
where the time goes in v3:
time: 39.5 us; the launch traced here: 39.3 us
  Pallas kernels  38.7 us (98%)
  between operations  0.64 us (2%)
    pallas_call x1, Pallas kernels, per_device(): pl.pallas_call(lambda *refs: step_kernel(width, height, *refs), out_shape...  36.7 us
    pallas_call x1, Pallas kernels, per_device(): pl.pallas_call(lambda *refs: update_kernel(width, height, *refs), out_sha...  1.97 us

profile of v3, /device:TPU:0, one launch (start us, length us, event | category | flops | bytes accessed | tf_op | source)
XLA Modules:
  0.0 39.3 jit_solution(17530847874471951031)
XLA Ops:
  0.6 36.7 %splat_gradients.1.refs_2_ = f32[4,9,128]{2,1,0:T(8,128)} custom-call(s32[16]{0:T(128)} %bitcast.7, f32[4,6]{1,0:T(4,128)} %refs_0_.1, f32[59,128]{1,0:T(8,128)} %refs_3_.1, s32[16,256]{1,0:T(8,128)} %bitcast.6, f32[3,16,256]{2,1,0:T(8,128)} %bitcast.5), custom_call_target="tpu_custom_call" | custom-call | tf_op jit(solution)/shard_map/splat_gradients/pallas_call | solution.py:647
  37.3 2.0 %update_gaussians.1 = (f32[59,128]{1,0:T(8,128)}, f32[59,128]{1,0:T(8,128)}, f32[59,128]{1,0:T(8,128)}) custom-call(f32[4,6]{1,0:T(4,128)} %refs_0_.1, f32[59,1]{1,0:T(8,128)} %constant.2.clone.refs_1_, f32[4,9,128]{2,1,0:T(8,128)} %splat_gradients.1.refs_2_, f32[59,128]{1,0:T(8,128)} %refs_3_.1, f32[59,128]{1,0:T(8,128)} %refs_4_.1, f32[59,128]{1,0:T(8,128)} %refs_5_.1), custom_call_target="tpu_custom_call" | custom-call | tf_op jit(solution)/shard_map/update_gaussians/pallas_call | solution.py:691

commit v4 on v3

--- a/solution.py
+++ b/solution.py
@@ -170,10 +170,8 @@
     return [lax.rem(start + step, count) for step in range(count)]
 
 
-def greet(views, tiles):
+def greet(others):
     barrier = pltpu.get_barrier_semaphore()
-    here = (views[0], tiles[0])
-    others = [(view, here[1]) for view in views[1:]] + [(here[0], tile) for tile in tiles[1:]]
     for device in others:
         pl.semaphore_signal(
             barrier, inc=1, device_id=device, device_id_type=pl.DeviceIdType.MESH
@@ -229,15 +227,10 @@
     table_ref,
     dense_ref,
     landing_ref,
-    summed_ref,
-    view_send,
-    view_recv,
-    tile_send,
-    tile_recv,
-    view_send_back,
-    view_recv_back,
-    tile_send_back,
-    tile_recv_back,
+    rows_send,
+    rows_recv,
+    grads_send,
+    grads_recv,
     picked,
     keeps,
     suffix,
@@ -268,7 +261,8 @@
     ]
     for fetch in fetches:
         fetch.start()
-    everyone_here = greet(views, tiles)
+    steps = [(turn, step) for step in range(tile_groups) for turn in range(view_count)][1:]
+    everyone_here = greet([(views[turn], tiles[step]) for turn, step in steps])
     for fetch in fetches[:2]:
         fetch.wait()
     values = [params_ref[at : at + 1, :] for at in range(59)]
@@ -279,31 +273,24 @@
     for row_at, value in enumerate(made[:5] + (opacities,) + made[5:]):
         rows_ref[:, row_at, :] = value
     everyone_here()
-    mine = table_ref.at[tiles[0]]
-    over_views = [
+    sent_rows = [
         send(
-            rows_ref.at[view],
-            mine.at[views[0]],
-            view_send.at[at],
-            view_recv.at[at],
-            (view, tiles[0]),
+            rows_ref.at[views[turn]],
+            table_ref.at[tiles[0], views[0]],
+            rows_send.at[turn, step],
+            rows_recv.at[turn, step],
+            (views[turn], tiles[step]),
         )
-        for at, view in enumerate(views[1:])
+        for turn, step in steps
     ]
     table_ref[pl.ds(tiles[0], 1), pl.ds(views[0], 1)] = rows_ref[pl.ds(views[0], 1)][None]
-    for copy in over_views:
-        copy.wait()
-    over_tiles = [
-        send(mine, mine, tile_send.at[at], tile_recv.at[at], (views[0], tile))
-        for at, tile in enumerate(tiles[1:])
-    ]
 
     row_ids = lax.broadcasted_iota(jnp.int32, (list_size, list_size), 0)
     col_ids = lax.broadcasted_iota(jnp.int32, (list_size, list_size), 1)
     for piece in range(2):
         here = slice(piece * list_size, (piece + 1) * list_size)
         before[here, :] = (row_ids < col_ids).astype(f32).astype(bf16)
-        after[here, :] = (row_ids > col_ids).astype(f32).astype(bf16)
+    after[...] = (row_ids > col_ids).astype(f32).astype(bf16)
     spread[...] = jnp.zeros_like(spread)
     tints[...] = jnp.zeros_like(tints)
     paints[...] = jnp.zeros_like(paints)
@@ -347,25 +334,32 @@
                         carry[slot] = jnp.where(mask, got, carry[slot])
         return tuple(carry)
 
-    def gather_arrived(at, carry):
-        source = lax.rem(tiles[0] + tile_groups - at, tile_groups)
+    def wait_rows(turn, step, source):
+        sender = (views[(view_count - turn) % view_count], source)
         pltpu.make_async_remote_copy(
-            src_ref=mine,
-            dst_ref=table_ref.at[source],
-            send_sem=tile_send.at[at - 1],
-            recv_sem=tile_recv.at[at - 1],
-            device_id=(views[0], source),
+            src_ref=rows_ref.at[sender[0]],
+            dst_ref=table_ref.at[source, sender[0]],
+            send_sem=rows_send.at[turn, step],
+            recv_sem=rows_recv.at[turn, step],
+            device_id=sender,
             device_id_type=pl.DeviceIdType.MESH,
         ).wait_recv()
+
+    def gather_arrived(step, carry):
+        source = lax.rem(tiles[0] + tile_groups - step, tile_groups)
+        for turn in range(view_count):
+            wait_rows(turn, step, source)
         return gather_from(source, carry)
 
+    for turn in range(1, view_count):
+        wait_rows(turn, 0, tiles[0])
     gathered = tuple(jnp.zeros((tile_dev, 128), f32) for _ in range(halves * 9))
     gathered = gather_from(tiles[0], gathered)
     gathered = lax.fori_loop(1, tile_groups, gather_arrived, gathered)
     for half in range(halves):
         for row_at in range(9):
             picked[row_at, :, half * 128 : half * 128 + 128] = gathered[half * 9 + row_at]
-    for copy in over_tiles:
+    for copy in sent_rows:
         copy.wait_send()
     group = spread.shape[1] // 32
     pair = keeps.shape[0]
@@ -443,9 +437,7 @@
     def flows_of(slot, tinted):
         for here in lines:
             flow = weight_s[slot, here, :] * tinted[here]
-            high, low = split(flow)
-            suffix[slot, here, 0:list_size] = high
-            suffix[slot, here, list_size : 2 * list_size] = low
+            suffix[slot, here, :] = flow.astype(bf16)
             flow_s[slot, here, :] = flow
 
     def grads_of(slot, rows, delta_x, top, behind, color_sums):
@@ -551,34 +543,25 @@
     else:
         lax.fori_loop(0, spread.shape[0], finish_group, 0)
 
-    over_tiles = [
+    sent_grads = [
         send(
-            dense_ref.at[tile],
-            landing_ref.at[at],
-            tile_send_back.at[at],
-            tile_recv_back.at[at],
-            (views[0], tile),
+            dense_ref.at[tiles[step], views[turn]],
+            landing_ref.at[turn, step],
+            grads_send.at[turn, step],
+            grads_recv.at[turn, step],
+            (views[turn], tiles[step]),
         )
-        for at, tile in enumerate(tiles[1:])
-    ]
-    total = dense_ref[pl.ds(tiles[0], 1)][0]
-    for at, copy in enumerate(over_tiles):
+        for turn, step in steps
+    ]
+    totals = [None] * view_count
+    totals[0] = dense_ref[pl.ds(tiles[0], 1), pl.ds(views[0], 1)][0, 0]
+    for copy, (turn, step) in zip(sent_grads, steps):
         copy.wait()
-        total = total + landing_ref[at]
-    summed_ref[...] = total
-    over_views = [
-        send(
-            summed_ref.at[view],
-            out_ref.at[views[0]],
-            view_send_back.at[at],
-            view_recv_back.at[at],
-            (view, tiles[0]),
-        )
-        for at, view in enumerate(views[1:])
-    ]
-    out_ref[pl.ds(views[0], 1)] = summed_ref[pl.ds(views[0], 1)]
-    for copy in over_views:
-        copy.wait()
+        block = landing_ref[turn, step]
+        totals[turn] = block if totals[turn] is None else totals[turn] + block
+    for turn in range(view_count):
+        sender = views[(view_count - turn) % view_count]
+        out_ref[pl.ds(sender, 1)] = totals[turn][None]
 
 
 def update_kernel(
@@ -633,12 +616,7 @@
     limit = 56 * 1024 * 1024
 
     dma = pltpu.SemaphoreType.DMA
-    semaphores = [
-        dma((view_count,)),
-        dma((view_count,)),
-        dma((tile_groups,)),
-        dma((tile_groups,)),
-    ]
+    semaphores = [dma((view_count, tile_groups))] * 4
     by_owner = (tile_groups, view_count, 9, owned)
     block_rows = (view_count, 9, owned)
     blocks = peers * owned // 256
@@ -659,17 +637,15 @@
             pltpu.VMEM(block_rows, f32),
             pltpu.VMEM(by_owner, f32),
             pltpu.VMEM(by_owner, f32),
-            pltpu.VMEM((tile_groups - 1,) + block_rows, f32),
-            pltpu.VMEM(block_rows, f32),
+            pltpu.VMEM((view_count, tile_groups, 9, owned), f32),
         ]
-        + semaphores
         + semaphores
         + [
             pltpu.VMEM((9, tile_dev, list_size), f32),
             pltpu.VMEM((pair, pixels, 2 * list_size), bf16),
-            pltpu.VMEM((pair, pixels, 2 * list_size), bf16),
+            pltpu.VMEM((pair, pixels, list_size), bf16),
             pltpu.VMEM((2 * list_size, list_size), bf16),
-            pltpu.VMEM((2 * list_size, list_size), bf16),
+            pltpu.VMEM((list_size, list_size), bf16),
             pltpu.VMEM((pair, pixels, list_size), f32),
             pltpu.VMEM((pair, pixels, list_size), f32),
             pltpu.VMEM((pair, pixels, list_size), f32),

time: 39.5 us -> 37 us (0.937)
  Pallas kernels: 38.7 us -> 35.9 us
    pallas_call x1, Pallas kernels: 36.7 us -> 33.9 us  [per_device(): pl.pallas_call(lambda *refs: step_kernel(width, height, *refs), out_shape...]
where the time goes in v4:
time: 37 us; the launch traced here: 36.5 us
  Pallas kernels  35.9 us (97%)
  between operations  0.64 us (2%)
    pallas_call x1, Pallas kernels, per_device(): pl.pallas_call(lambda *refs: step_kernel(width, height, *refs), out_shape...  33.9 us
    pallas_call x1, Pallas kernels, per_device(): pl.pallas_call(lambda *refs: update_kernel(width, height, *refs), out_sha...  1.97 us

profile of v4, /device:TPU:0, one launch (start us, length us, event | category | flops | bytes accessed | tf_op | source)
XLA Modules:
  0.0 36.5 jit_solution(17630681041904446438)
XLA Ops:
  0.6 33.9 %splat_gradients.1.refs_2_ = f32[4,9,128]{2,1,0:T(8,128)} custom-call(s32[16]{0:T(128)} %bitcast.7, f32[4,6]{1,0:T(4,128)} %refs_0_.1, f32[59,128]{1,0:T(8,128)} %refs_3_.1, s32[16,256]{1,0:T(8,128)} %bitcast.6, f32[3,16,256]{2,1,0:T(8,128)} %bitcast.5), custom_call_target="tpu_custom_call" | custom-call | tf_op jit(solution)/shard_map/splat_gradients/pallas_call | solution.py:625
  34.6 2.0 %update_gaussians.1 = (f32[59,128]{1,0:T(8,128)}, f32[59,128]{1,0:T(8,128)}, f32[59,128]{1,0:T(8,128)}) custom-call(f32[4,6]{1,0:T(4,128)} %refs_0_.1, f32[59,1]{1,0:T(8,128)} %constant.2.clone.refs_1_, f32[4,9,128]{2,1,0:T(8,128)} %splat_gradients.1.refs_2_, f32[59,128]{1,0:T(8,128)} %refs_3_.1, f32[59,128]{1,0:T(8,128)} %refs_4_.1, f32[59,128]{1,0:T(8,128)} %refs_5_.1), custom_call_target="tpu_custom_call" | custom-call | tf_op jit(solution)/shard_map/update_gaussians/pallas_call | solution.py:667

commit v5 on v4

--- a/solution.py
+++ b/solution.py
@@ -294,14 +294,14 @@
     spread[...] = jnp.zeros_like(spread)
     tints[...] = jnp.zeros_like(tints)
     paints[...] = jnp.zeros_like(paints)
-    painted[:, :, 3 * list_size :] = jnp.zeros(
+    painted[:, :, 2 * list_size :] = jnp.zeros(
         (painted.shape[0], painted.shape[1], 128), bf16
     )
     channels = lax.broadcasted_iota(jnp.int32, (16, 128), 0)
     pieces_at = lax.broadcasted_iota(jnp.int32, (16, 128), 1)
     same = (channels % 3 == pieces_at % 3) & (channels < 9) & (pieces_at < 9)
     for slot in range(paints.shape[0]):
-        paints[slot, 0:16, 3 * list_size :] = jnp.where(same, -1.0, 0.0).astype(bf16)
+        paints[slot, 0:16, 2 * list_size :] = jnp.where(same, -1.0, 0.0).astype(bf16)
     lane_ids = lax.broadcasted_iota(jnp.int32, (1, list_size), 1)
     pixel_ids = lax.broadcasted_iota(jnp.int32, (16, list_size), 0).astype(f32)
     column_ids = lax.broadcasted_iota(jnp.int32, (256, list_size), 0)
@@ -406,7 +406,7 @@
         lows = jnp.concatenate([middle, middle, middle, empty], axis=0).astype(bf16)
         paints[slot, 0:16, 0:list_size] = highs
         paints[slot, 0:16, list_size : 2 * list_size] = highs
-        paints[slot, 0:16, 2 * list_size : 3 * list_size] = lows
+        paints[slot, 64:80, 0:list_size] = lows
         tints[slot, 0:16, :] = jnp.concatenate([high, middle, low, empty], axis=0).astype(bf16)
         wanted = jnp.concatenate(
             [target_ref[channel, pl.ds(tile_at, 1), :] for channel in range(3)], axis=0
@@ -415,7 +415,7 @@
         middle = (wanted - high).astype(bf16).astype(f32)
         low = wanted - high - middle
         wanted = jnp.concatenate([high, middle, low, jnp.zeros((7, wanted.shape[1]), f32)], axis=0)
-        painted[slot, :, 3 * list_size : 3 * list_size + 16] = wanted.T.astype(bf16)
+        painted[slot, :, 2 * list_size : 2 * list_size + 16] = wanted.T.astype(bf16)
 
     def weights_of(slot, passed):
         for here in lines:
@@ -424,7 +424,6 @@
             weight_s[slot, here, :] = weight
             painted[slot, here, 0:list_size] = high
             painted[slot, here, list_size : 2 * list_size] = low
-            painted[slot, here, 2 * list_size : 3 * list_size] = high
 
     def signs_of(gaps):
         return jnp.where(gaps > 0.0, 1.0, jnp.where(gaps < 0.0, -1.0, 0.0))
@@ -487,7 +486,7 @@
                 )
             )
         for slot in slots:
-            signs = signs_of(gaps[slot])
+            signs = signs_of(gaps[slot] + pltpu.roll(gaps[slot], 64, 1))
             tinted.append(jnp.dot(signs.astype(bf16), tints[slot], preferred_element_type=f32))
             color_sums.append(color_grads(slot, signs))
         for slot in slots:
@@ -621,7 +620,7 @@
     block_rows = (view_count, 9, owned)
     blocks = peers * owned // 256
     group = 16
-    pair = 2
+    pair = 8
     row_grads = pl.pallas_call(
         lambda *refs: step_kernel(width, height, *refs),
         out_shape=jax.ShapeDtypeStruct(block_rows, f32),
@@ -650,8 +649,8 @@
             pltpu.VMEM((pair, pixels, list_size), f32),
             pltpu.VMEM((pair, pixels, list_size), f32),
             pltpu.VMEM((pair, pixels, list_size), f32),
-            pltpu.VMEM((pair, pixels, 3 * list_size + 128), bf16),
-            pltpu.VMEM((pair, 128, 3 * list_size + 128), bf16),
+            pltpu.VMEM((pair, pixels, 2 * list_size + 128), bf16),
+            pltpu.VMEM((pair, 128, 2 * list_size + 128), bf16),
             pltpu.VMEM((pair, 128, list_size), bf16),
             pltpu.VMEM((group * 32, pair * list_size), bf16),
             pltpu.VMEM((256, pair * list_size), bf16),

time: 37 us -> 33.7 us (0.911)
  Pallas kernels: 35.9 us -> 32.6 us
    pallas_call x1, Pallas kernels: 33.9 us -> 30.6 us  [per_device(): pl.pallas_call(lambda *refs: step_kernel(width, height, *refs), out_shape...]
where the time goes in v5:
time: 33.7 us; the launch traced here: 33.2 us
  Pallas kernels  32.6 us (97%)
  between operations  0.64 us (2%)
    pallas_call x1, Pallas kernels, per_device(): pl.pallas_call(lambda *refs: step_kernel(width, height, *refs), out_shape...  30.6 us
    pallas_call x1, Pallas kernels, per_device(): pl.pallas_call(lambda *refs: update_kernel(width, height, *refs), out_sha...  1.97 us

profile of v5, /device:TPU:0, one launch (start us, length us, event | category | flops | bytes accessed | tf_op | source)
XLA Modules:
  0.0 33.2 jit_solution(9474724638712990107)
XLA Ops:
  0.6 30.6 %splat_gradients.1.refs_2_ = f32[4,9,128]{2,1,0:T(8,128)} custom-call(s32[16]{0:T(128)} %bitcast.7, f32[4,6]{1,0:T(4,128)} %refs_0_.1, f32[59,128]{1,0:T(8,128)} %refs_3_.1, s32[16,256]{1,0:T(8,128)} %bitcast.6, f32[3,16,256]{2,1,0:T(8,128)} %bitcast.5), custom_call_target="tpu_custom_call" | custom-call | tf_op jit(solution)/shard_map/splat_gradients/pallas_call | solution.py:624
  31.3 2.0 %update_gaussians.1 = (f32[59,128]{1,0:T(8,128)}, f32[59,128]{1,0:T(8,128)}, f32[59,128]{1,0:T(8,128)}) custom-call(f32[4,6]{1,0:T(4,128)} %refs_0_.1, f32[59,1]{1,0:T(8,128)} %constant.2.clone.refs_1_, f32[4,9,128]{2,1,0:T(8,128)} %splat_gradients.1.refs_2_, f32[59,128]{1,0:T(8,128)} %refs_3_.1, f32[59,128]{1,0:T(8,128)} %refs_4_.1, f32[59,128]{1,0:T(8,128)} %refs_5_.1), custom_call_target="tpu_custom_call" | custom-call | tf_op jit(solution)/shard_map/update_gaussians/pallas_call | solution.py:666
